TPU v7x, 256 devices: a whole 4x4x8 slice. The times are simulated.
256 devices in a mesh: fsdp: 64 (over x, y_hi, z), tp: 4 (over y_lo, core).
Axes of the slice: x: 4, y: 4 (y_hi: 2, y_lo: 2; y = y_hi * 2 + y_lo), z: 8, core: 2. Of those that a mesh axis runs over, the one named last changes fastest.
Arguments:
- weight_master: float32 [5120, 7168], P('fsdp', 'tp'), may hold values from -0.078125 to 0.078125
- gradient: float32 [5120, 7168], P('fsdp', 'tp'), may hold values from -6 to 6
- first_moment: float32 [5120, 7168], P('fsdp', 'tp'), may hold values from -2 to 2
- second_moment: float32 [5120, 7168], P('fsdp', 'tp'), may hold values from 0.02 to 0.2
- query_key_value_bias: bfloat16 [7168], P('tp'), may hold values from -3 to 3
- new_tokens: bfloat16 [4, 3072, 5120], P(None, 'fsdp', 'tp'), may hold values from -6 to 6
- norm_gain: bfloat16 [5120], P('tp'), may hold values from 0.25 to 1.75
- cache_len: int32 [3072], replicated, may hold values from 1 to 160, as said below
- key_cache: bfloat16 [64, 4, 96, 160, 128], P('fsdp', 'tp'), may hold values from -700 to 700
- value_cache: bfloat16 [64, 4, 96, 160, 128], P('fsdp', 'tp'), may hold values from -6 to 6
Outputs:
- new_master: float32 [5120, 7168], P('fsdp', 'tp')
- new_first: float32 [5120, 7168], P('fsdp', 'tp')
- new_second: float32 [5120, 7168], P('fsdp', 'tp')
- context: bfloat16 [4, 3072, 5120], P(None, 'fsdp', 'tp')
Inputs may be any that keep to these rules, and one draw needn't show every extreme that they name: `cache_len`: among the 48 rows of each index of fsdp one has a full cache.
All inputs are finite; a program needn't handle non-finite values.
Results may differ from a plain program's by a relative error of at most 0.015.
The roundings to bfloat16 on the way count: a program that leaves them out, or rounds other values in their place, can miss the bound.
Values may be sent and summed in bfloat16 or wider, within the bound.
A program may use at most 128 MiB of HBM per device.

v0:
```python
import jax
import jax.numpy as jnp
from jax import lax
from jax.sharding import PartitionSpec as P

BETA_ONE = 0.9
BETA_TWO = 0.95
LEARN_RATE = 0.002
ADAM_EPS = 1e-08
CORR_ONE = 1.0 - 0.9**10
CORR_TWO = 1.0 - 0.95**10
NORM_EPS = 1e-06
ROPE_BASE = 1000000.0


def partner(block, axis, stride):
    count = lax.axis_size(axis)
    route = []
    for low in range(count):
        high = low | 1 << stride
        if high != low and high < count:
            route += [(low, high), (high, low)]
    return lax.ppermute(block, axis, route)


def adam_update(weight_master, gradient, first_moment, second_moment):
    new_first = BETA_ONE * first_moment + (1.0 - BETA_ONE) * gradient
    new_second = BETA_TWO * second_moment + (1.0 - BETA_TWO) * gradient * gradient
    step_size = new_first / CORR_ONE / (jnp.sqrt(new_second / CORR_TWO) + ADAM_EPS)
    return (weight_master - LEARN_RATE * step_size, new_first, new_second)


def rms_scale(tokens, gain_row):
    floats = tokens.astype(jnp.float32)
    inverse = lax.rsqrt(jnp.mean(floats * floats, axis=-1, keepdims=True) + NORM_EPS)
    return (floats * inverse * gain_row.astype(jnp.float32)).astype(jnp.bfloat16)


def rotate(values, positions):
    half_width = values.shape[-1] // 2
    inverse = jnp.power(
        ROPE_BASE, -jnp.arange(half_width, dtype=jnp.float32) * (2.0 / (2 * half_width))
    )
    angles = positions.astype(jnp.float32)[..., None] * inverse
    cosine = jnp.cos(angles)
    sine_part = jnp.sin(angles)
    first_part = values[..., :half_width]
    second_part = values[..., half_width:]
    return jnp.concatenate(
        [
            first_part * cosine - second_part * sine_part,
            second_part * cosine + first_part * sine_part,
        ],
        axis=-1,
    )


def attend(queries, keys_new, values_new, cached_keys, cached_values, lengths):
    score_scale = 1.0 / jnp.sqrt(jnp.float32(queries.shape[-1]))
    cached_scores = (
        jnp.einsum("srbph,brlh->srbpl", queries, cached_keys, preferred_element_type=jnp.float32)
        * score_scale
    )
    position = jnp.arange(cached_keys.shape[2], dtype=jnp.int32)
    valid_mask = position[None, :] < lengths[:, None]
    cached_scores = jnp.where(valid_mask[None, :, None, None, :], cached_scores, -jnp.inf)
    fresh_scores = (
        jnp.einsum("srbph,trbh->srbpt", queries, keys_new, preferred_element_type=jnp.float32)
        * score_scale
    )
    steps_here = queries.shape[0]
    causal = jnp.arange(steps_here)[:, None] >= jnp.arange(steps_here)[None, :]
    fresh_scores = jnp.where(causal[:, None, None, None, :], fresh_scores, -jnp.inf)
    row_max = jnp.maximum(jnp.max(cached_scores, axis=-1), jnp.max(fresh_scores, axis=-1))
    cached_exp = jnp.exp(cached_scores - row_max[..., None])
    fresh_exp = jnp.exp(fresh_scores - row_max[..., None])
    row_total = jnp.sum(cached_exp, axis=-1) + jnp.sum(fresh_exp, axis=-1)
    cached_prob = (cached_exp / row_total[..., None]).astype(jnp.bfloat16)
    fresh_prob = (fresh_exp / row_total[..., None]).astype(jnp.bfloat16)
    mixed = jnp.einsum(
        "srbpl,brlh->srbph", cached_prob, cached_values, preferred_element_type=jnp.float32
    )
    mixed = mixed + jnp.einsum(
        "srbpt,trbh->srbph", fresh_prob, values_new, preferred_element_type=jnp.float32
    )
    return mixed.astype(jnp.bfloat16)


def on_device(
    weight_master,
    gradient,
    first_moment,
    second_moment,
    query_key_value_bias,
    new_tokens,
    norm_gain,
    cache_len,
    key_cache,
    value_cache,
):
    new_master, new_first, new_second = adam_update(
        weight_master, gradient, first_moment, second_moment
    )
    narrow = new_master.astype(jnp.bfloat16)
    half_cols = narrow.shape[1] // 2
    fsdp_index = lax.axis_index("fsdp")
    parity = fsdp_index % 2
    gathered = lax.all_gather(narrow, "fsdp", axis=0, tiled=True)
    own_weight = lax.dynamic_slice_in_dim(gathered, parity * half_cols, half_cols, 1)
    own_bias = lax.dynamic_slice_in_dim(query_key_value_bias, parity * half_cols, half_cols, 0)
    full_tokens, full_gain = (
        lax.all_gather(new_tokens, "tp", axis=2, tiled=True),
        lax.all_gather(norm_gain, "tp", axis=0, tiled=True),
    )
    other_tokens = partner(full_tokens, "fsdp", 0)
    is_first = parity == 0
    group_tokens = jnp.concatenate(
        [
            jnp.where(is_first, full_tokens, other_tokens),
            jnp.where(is_first, other_tokens, full_tokens),
        ],
        axis=1,
    )
    steps_here, group_rows, model_width = group_tokens.shape
    group_start = fsdp_index // 2 * group_rows
    group_len = lax.dynamic_slice_in_dim(cache_len, group_start, group_rows, 0)
    normed = rms_scale(group_tokens, full_gain)
    joined_projection = jnp.dot(
        normed.reshape(steps_here * group_rows, model_width),
        own_weight,
        preferred_element_type=jnp.float32,
    )
    joined_projection = joined_projection + own_bias.astype(jnp.float32)
    head_dim = key_cache.shape[-1]
    per_group = half_cols // head_dim
    joined_projection = joined_projection.reshape(steps_here, group_rows, 1, per_group, head_dim)
    positions = group_len[None, :] + jnp.arange(steps_here, dtype=jnp.int32)[:, None]
    queries = rotate(
        joined_projection[:, :, :, : per_group - 2], positions[:, :, None, None]
    ).astype(jnp.bfloat16)
    keys_new = rotate(joined_projection[:, :, :, per_group - 2], positions[:, :, None]).astype(
        jnp.bfloat16
    )
    values_new = joined_projection[:, :, :, per_group - 1].astype(jnp.bfloat16)
    attended = attend(queries, keys_new, values_new, key_cache[0], value_cache[0], group_len)
    attended = attended.reshape(steps_here, group_rows, (per_group - 2) * head_dim)
    own_count = group_rows // 2
    own_context = lax.dynamic_slice_in_dim(attended, parity * own_count, own_count, 1)
    their_context = lax.dynamic_slice_in_dim(attended, (1 - parity) * own_count, own_count, 1)
    returned = partner(their_context, "fsdp", 0)
    output = jnp.concatenate(
        [jnp.where(is_first, own_context, returned), jnp.where(is_first, returned, own_context)],
        axis=2,
    )
    return (new_master, new_first, new_second, output)


def solution(mesh):
    in_specs = (
        P("fsdp", "tp"),
        P("fsdp", "tp"),
        P("fsdp", "tp"),
        P("fsdp", "tp"),
        P("tp"),
        P(None, "fsdp", "tp"),
        P("tp"),
        P(),
        P("fsdp", "tp", None, None, None),
        P("fsdp", "tp", None, None, None),
    )
    out_specs = (P("fsdp", "tp"), P("fsdp", "tp"), P("fsdp", "tp"), P(None, "fsdp", "tp"))
    return jax.shard_map(
        on_device, mesh=mesh, in_specs=in_specs, out_specs=out_specs, check_vma=False
    )
```

profile of v0, /device:TPU:32, one launch (start us, length us, event | category | flops | bytes accessed | tf_op | source)
XLA Modules:
  0.0 300.0 jit_solution(3811939136019201400)
XLA Ops:
  7.2 0.0 all-gather.4.cloned.1.call-start
  7.2 0.7 all-gather.4.cloned.1.call-update
  7.9 0.0 all-gather.6.cloned.1.call-start
  8.0 3.1 %fusion.48 = (bf16[80,1792]{1,0:T(8,128)(2,1)}, f32[80,1792]{1,0:T(8,128)}, f32[80,1792]{1,0:T(8,128)}, f32[80,1792]{1,0:T(8,128)}) fusion(f32[80,1792]{1,0:T(8,128)} %param.10, f32[80,1792]{1,0:T(8,128)} %param.11, f32[80,1792]{1,0:T(8,128)} %param.12, f32[80,1792]{1,0:T(8,128)} %param.13), kind=kLoop, calls=%fused_computation.80 | loop fusion | flops 2007040 | bytes 4300800 | tf_op jit(solution)/shard_map/convert_element_type | solution.py:104
  11.1 0.0 all-gather.6.cloned.1.call-update
  11.1 31.8 %all-gather.4.cloned.1.call-done = bf16[4,48,5120]{2,1,0:T(8,128)(2,1)} async-done(((bf16[4,48,1280]{2,1,0:T(8,128)(2,1)}), bf16[4,48,5120]{2,1,0:T(8,128)(2,1)}) %all-gather.4.cloned.1.call-update) | async-done | bytes 1966096 | tf_op jit(solution)/shard_map/all_gather | solution.py:112
  42.9 0.5 collective-permute-start
  43.4 5.2 %all-gather = bf16[4,1,1280]{2,1,0:T(2,128)(2,1)S(1)} all-gather(bf16[1,1,1280]{2,1,0:T(2,128)(2,1)S(1)} %reshape.259), channel_id=1, replica_groups=mesh['fsdp'=64,'tp'=4] {'tp'}, dimensions={0}, use_global_device_ids=true | all-gather | bytes 12800 | tf_op jit(solution)/shard_map/all_gather | solution.py:113
  48.7 0.8 dynamic_slice.15
  49.5 0.1 dynamic-slice_convert_fusion
  49.5 0.1 iota_compare_fusion
  49.6 0.1 add_convert_fusion.1
  49.7 1.6 multiply_cosine_fusion.1
  51.4 44.2 %collective-permute-done = bf16[4,48,5120]{2,1,0:T(8,128)(2,1)} collective-permute-done((bf16[4,48,5120]{2,1,0:T(8,128)(2,1)}, bf16[4,48,5120]{2,1,0:T(8,128)(2,1)}, u32[]{:S(2)}, u32[]{:S(2)}) %collective-permute-start) | collective-permute-done | bytes 1966112 | tf_op jit(solution)/shard_map/ppermute | solution.py:23
  95.5 2.4 broadcast_select_fusion.1
  97.9 1.3 copy-done
  99.2 0.9 multiply_reduce_fusion
  100.1 0.1 rsqrt.12
  100.2 2.6 maximum_convert_fusion
  102.7 3.3 %fusion.3 = bf16[384,5120]{1,0:T(8,128)(2,1)} fusion(f32[4,96,5120]{2,1,0:T(8,128)S(1)} %maximum_convert_fusion, f32[5120]{0:T(1024)S(1)} %bitcast.101, f32[384]{0:T(512)S(1)} %rsqrt.12), kind=kLoop, calls=%fused_computation.4 | loop fusion | flops 5898240 | bytes 11818496 | tf_op jit(solution)/shard_map/convert_element_type | solution.py:36
  106.0 151.3 %all-gather.6.cloned.1.call-done = bf16[5120,1792]{1,0:T(8,128)(2,1)} async-done(((bf16[80,1792]{1,0:T(8,128)(2,1)}), bf16[5120,1792]{1,0:T(8,128)(2,1)}) %all-gather.6.cloned.1.call-update) | async-done | bytes 18350096 | tf_op jit(solution)/shard_map/all_gather | solution.py:108
  257.3 9.7 %fusion.17 = f32[384,896]{1,0:T(8,128)S(1)} fusion(bf16[384,5120]{1,0:T(8,128)(2,1)} %fusion.3, bf16[5120,1792]{1,0:T(8,128)(2,1)} %all-gather.6.cloned.1.call-done, s32[]{:T(128)S(6)} %select_n.66, f32[896]{0:T(1024)S(1)} %dynamic-slice_convert_fusion), kind=kOutput, calls=%fused_computation.28 | convolution fusion | flops 3523559424 | bytes 14487044 | tf_op jit(solution)/shard_map/dot_general | solution.py:128
  267.0 0.2 reshape.252
  267.2 0.5 fusion.50
  267.7 0.2 slice.30
  267.9 0.2 slice.33
  268.1 0.1 copy.61
  268.3 2.0 fusion.42
  270.2 0.4 fusion.23
  270.6 2.6 fusion.10
  273.2 3.8 %fusion.51 = (f32[4,96,5]{2,0,1:T(4,128)S(1)}, f32[4,96,1,5,4]{3,4,0,1,2:T(4,128)S(1)}) fusion(bf16[4,96,5,64]{3,2,0,1:T(8,128)(2,1)S(1)} %get-tuple-element.15, bf16[4,96,5,64]{3,2,0,1:T(8,128)(2,1)S(1)} %get-tuple-element.14, bf16[4,96,64]{2,0,1:T(4,128)(2,1)S(1)} %get-tuple-element.21, bf16[4,96,64]{2,0,1:T(4,128)(2,1)S(1)} %get-tuple-element.20, ...), kind=kOutput, calls=%fused_computation.82 | convolution fusion | flops 3166848 | bytes 628240 | tf_op jit(solution)/shard_map/srbph,trbh->srbpt/dot_general | solution.py:68
  277.0 0.0 copy-start.4
  277.0 0.1 max.9
  277.1 0.7 fusion.25
  277.8 1.5 fusion.9
  279.3 0.1 add.109
  279.4 2.0 fusion.4
  281.4 0.7 fusion.21
  282.1 0.7 copy.30
  282.8 0.2 constant_dynamic-slice_fusion
  283.0 0.2 copy.31
  283.3 2.3 collective-permute-start.1
  285.6 5.5 %collective-permute-done.1 = bf16[4,48,640]{2,1,0:T(8,128)(2,1)S(1)} collective-permute-done((bf16[4,48,640]{2,1,0:T(8,128)(2,1)S(1)}, bf16[4,48,640]{2,1,0:T(8,128)(2,1)S(1)}, u32[]{:S(2)}, u32[]{:S(2)}) %collective-permute-start.1) | collective-permute-done | bytes 245792 | tf_op jit(solution)/shard_map/ppermute | solution.py:23
  291.1 0.3 copy.32
  291.4 0.4 broadcast_select_fusion.3
  291.8 0.2 copy.34
  292.1 0.2 copy.35
  292.3 0.8 pad_maximum_fusion.1
  (13 shorter events, 0.1 us)
Async XLA Ops:
  7.2 36.2 %copy-start.2 = (bf16[1280]{0:T(1024)(128)(2,1)S(1)}, bf16[1280]{0:T(1024)(128)(2,1)}, u32[]{:S(2)}) copy-start(bf16[1280]{0:T(1024)(128)(2,1)} %param.16) | copy-start | bytes 7684
  7.2 42.3 %copy-start.3 = (bf16[1792]{0:T(1024)(128)(2,1)S(1)}, bf16[1792]{0:T(1024)(128)(2,1)}, u32[]{:S(2)}) copy-start(bf16[1792]{0:T(1024)(128)(2,1)} %param.14) | copy-start | bytes 10756
  7.2 35.7 %all-gather.4.cloned.1.call-start = ((), (), s32[]{:S(2)}) async-start(), calls=%async_computation | async-start | bytes 2457600 | tf_op jit(solution)/shard_map/all_gather | solution.py:112
  7.9 249.4 %all-gather.6.cloned.1.call-start = ((), (), s32[]{:S(2)}) async-start(), calls=%async_computation.1 | async-start | bytes 18636800 | tf_op jit(solution)/shard_map/all_gather | solution.py:108
  42.9 52.6 %collective-permute-start = (bf16[4,48,5120]{2,1,0:T(8,128)(2,1)}, bf16[4,48,5120]{2,1,0:T(8,128)(2,1)}, u32[]{:S(2)}, u32[]{:S(2)}) collective-permute-start(bf16[4,48,5120]{2,1,0:T(8,128)(2,1)} %all-gather.4.cloned.1.call-done), channel_id=1, source_target_pairs={{0,4},{4,0},{8,12},{12,8},{16,20},{20,16},{24,28},{28,24},{32,36},... | collective-permute-start | bytes 5898248 | tf_op jit(solution)/shard_map/ppermute | solution.py:23
  97.9 1.3 copy-start
  268.1 2.5 copy-start.1
  277.0 2.4 copy-start.4
  283.3 7.8 %collective-permute-start.1 = (bf16[4,48,640]{2,1,0:T(8,128)(2,1)S(1)}, bf16[4,48,640]{2,1,0:T(8,128)(2,1)S(1)}, u32[]{:S(2)}, u32[]{:S(2)}) collective-permute-start(bf16[4,48,640]{2,1,0:T(8,128)(2,1)S(1)} %copy.31), channel_id=1, source_target_pairs={{0,4},{4,0},{8,12},{12,8},{16,20},{20,16},{24,28},{28,24},{32,36},... | collective-permute-start | bytes 737288 | tf_op jit(solution)/shard_map/ppermute | solution.py:23
Sparse Core Ops, SparseCore 0:
  9.8 33.0 all-gather.3
  47.1 210.1 all-gather.5
where the time goes:
time: 302 us; the launch traced here: 300 us
  waiting for transfers between devices  233 us (77%)
  other arithmetic  20 us (7%)
  matrix products  18.7 us (6%)
  between operations  14.3 us (5%)
  local copies, waits for them, and re-layouts  5.4 us (2%)
  blocking collectives  5.19 us (2%)
    all_gather x1, waiting for transfers between devices, on_device(): gathered = lax.all_gather(narrow, 'fsdp', axis=0, tiled=True)  151 us
    ppermute x2, waiting for transfers between devices, partner(): return lax.ppermute(block, axis, route)  49.7 us
    all_gather x1, waiting for transfers between devices, on_device(): lax.all_gather(new_tokens, 'tp', axis=2, tiled=True)  31.8 us
    dot_general x1, matrix products, on_device(): jnp.dot(normed.reshape(steps_here * group_rows, model_width), own_weight,...  9.67 us
  transfers between devices with their start and end apart: 4, of which 4 were waited for; matrix products, arithmetic and copies ran while one was open for 5% of the time, Pallas kernels for 0%

commit v1 on v0

--- a/solution.py
+++ b/solution.py
@@ -1,6 +1,8 @@
 import jax
 import jax.numpy as jnp
 from jax import lax
+from jax.experimental import pallas as pl
+from jax.experimental.pallas import tpu as pltpu
 from jax.sharding import PartitionSpec as P
 
 BETA_ONE = 0.9
@@ -12,6 +14,10 @@
 NORM_EPS = 1e-06
 ROPE_BASE = 1000000.0
 
+MESH = pl.DeviceIdType.MESH
+NX, NH, NZ = 4, 2, 8
+NB = 4
+
 
 def partner(block, axis, stride):
     count = lax.axis_size(axis)
@@ -30,10 +36,250 @@
     return (weight_master - LEARN_RATE * step_size, new_first, new_second)
 
 
-def rms_scale(tokens, gain_row):
-    floats = tokens.astype(jnp.float32)
-    inverse = lax.rsqrt(jnp.mean(floats * floats, axis=-1, keepdims=True) + NORM_EPS)
-    return (floats * inverse * gain_row.astype(jnp.float32)).astype(jnp.bfloat16)
+def projection_kernel(
+    narrow, tokens, gain, out, W, A, N, ssq, psend, precv,
+    z_send, z_recv, x_send, x_recv, q_send, q_recv,
+    t_send, t_recv, s_send, s_recv, p_send, p_recv,
+):
+    heads, _, depth, lanes = W.shape
+    rows = depth // NZ
+    half = depth // 2
+    f = lax.axis_index("fsdp")
+    b = lax.axis_index("tp")
+    x, h, z = f // (NH * NZ), (f // NZ) % NH, f % NZ
+    lo, c = b // 2, b % 2
+    s = z % 2
+
+    def at(x_, h_, z_, lo_, c_):
+        return {"fsdp": (x_ * NH + h_) * NZ + z_, "tp": lo_ * 2 + c_}
+
+    x_up = at((x + 1) % NX, h, z, lo, c)
+    x_down = at((x + NX - 1) % NX, h, z, lo, c)
+    z_to = [at(x, h, (z + d) % NZ, lo, c) for d in range(NZ)]
+    z_pair = at(x, h, z + 1 - 2 * s, lo, c)
+    lo_pair = at(x, h, z, 1 - lo, c)
+    sibling = at(x, h, z, lo, 1 - c)
+    cross = at(x, h, z, 1 - lo, 1 - c)
+    h_far = at(x, 1 - h, z, lo, c)
+    h_near = at(x, 1 - h, z, 1 - lo, c)
+
+    barrier = pltpu.get_barrier_semaphore()
+    everyone = [x_up, x_down, lo_pair, sibling, cross, h_far, h_near] + z_to[1:]
+    for other in everyone:
+        pl.semaphore_signal(barrier, inc=1, device_id=other, device_id_type=MESH)
+
+    flat = tokens[...].astype(jnp.float32)
+    square = flat * flat
+    part = square[:, :lanes]
+    for k in range(1, square.shape[1] // lanes):
+        part = part + square[:, k * lanes : (k + 1) * lanes]
+    ssq[b] = part
+    pl.semaphore_wait(barrier, len(everyone))
+
+    sent = []
+
+    def send(src, dst, send_sem, recv_sem, to):
+        copy = pltpu.make_async_remote_copy(
+            src_ref=src, dst_ref=dst, send_sem=send_sem, recv_sem=recv_sem,
+            device_id=to, device_id_type=MESH,
+        )
+        copy.start()
+        sent.append(copy)
+
+    def arrive(dst, send_sem, recv_sem, to):
+        pltpu.make_async_remote_copy(
+            src_ref=dst, dst_ref=dst, send_sem=send_sem, recv_sem=recv_sem,
+            device_id=to, device_id_type=MESH,
+        ).wait_recv()
+
+    def w_rows(j, x_, z_):
+        return W.at[j, x_, pl.ds(pl.multiple_of(z_ * rows, 16), rows)]
+
+    def w_group(j, x_, g):
+        return W.at[j, x_, pl.ds(g * half, half)]
+
+    own_copies = {}
+
+    def z_out(j):
+        own = pltpu.make_async_copy(narrow.at[s * heads + j], w_rows(j, x, z), z_recv.at[j, 0])
+        own.start()
+        own_copies[j] = own
+        for d in (4, 3, 5, 2, 6, 1, 7):
+            parity = (s + d) % 2
+            send(narrow.at[parity * heads + j], w_rows(j, x, z), z_send.at[j, d],
+                 z_recv.at[j, d], z_to[d])
+
+    def x_out(j):
+        own_copies[j].wait()
+        for d in range(1, NZ):
+            arrive(w_rows(j, x, (z + NZ - d) % NZ), z_send.at[j, d], z_recv.at[j, d], z_to[d])
+        for g in (0, 1):
+            for k, to in ((0, x_up), (1, x_down)):
+                send(w_group(j, x, g), w_group(j, x, g), x_send.at[j, 2 * g + k],
+                     x_recv.at[j, 2 * g + k], to)
+
+    def x_on(j):
+        for g, k in ((0, 0), (1, 1), (0, 1), (1, 0)):
+            source = (x + NX - 1) % NX if k == 0 else (x + 1) % NX
+            to = x_up if k == 0 else x_down
+            arrive(w_group(j, source, g), x_send.at[j, 2 * g + k], x_recv.at[j, 2 * g + k], to)
+            if g == k:
+                send(w_group(j, source, g), w_group(j, source, g), x_send.at[j, 4 + g],
+                     x_recv.at[j, 4 + g], to)
+
+    def x_end(j):
+        for g in (0, 1):
+            arrive(w_group(j, (x + 2) % NX, g), x_send.at[j, 4 + g], x_recv.at[j, 4 + g],
+                   x_up if g == 0 else x_down)
+
+    def a_at(b_, h_, s_):
+        return A.at[b_, 2 * h_ + s_]
+
+    local = []
+    b_lo = (1 - lo) * 2 + c
+
+    def to_sibling(ref, kind, i):
+        send(ref, ref, s_send.at[kind, i], s_recv.at[kind, i], sibling)
+
+    def tokens_out(i, s_):
+        send(N.at[1 - h, s_], a_at(b, h, s_), t_send.at[0, i], t_recv.at[0, i], h_near)
+        send(N.at[h, s_], a_at(b, h, s_), t_send.at[1, i], t_recv.at[1, i], lo_pair)
+        own = pltpu.make_async_copy(N.at[h, s_], a_at(b, h, s_), t_recv.at[4, i])
+        own.start()
+        local.append(own)
+        send(N.at[h, s_], a_at(b, h, s_), s_send.at[0, i], s_recv.at[0, i], sibling)
+
+    def tokens_on(i, s_):
+        piece = a_at(b_lo, 1 - h, s_)
+        arrive(piece, t_send.at[0, i], t_recv.at[0, i], h_near)
+        send(piece, piece, t_send.at[2, i], t_recv.at[2, i], lo_pair)
+        to_sibling(piece, 1, i)
+        piece = a_at(b_lo, h, s_)
+        arrive(piece, t_send.at[1, i], t_recv.at[1, i], lo_pair)
+        to_sibling(piece, 2, i)
+
+    def tokens_last(i, s_):
+        piece = a_at(b, 1 - h, s_)
+        arrive(piece, t_send.at[2, i], t_recv.at[2, i], lo_pair)
+        to_sibling(piece, 3, i)
+
+    def tokens_end():
+        sib = lo * 2 + 1 - c
+        sib_lo = (1 - lo) * 2 + 1 - c
+        for i, s_ in ((0, s), (1, 1 - s)):
+            local[i].wait()
+            for kind, b_, h_ in ((0, sib, h), (1, sib_lo, 1 - h), (2, sib_lo, h), (3, sib, 1 - h)):
+                arrive(a_at(b_, h_, s_), s_send.at[kind, i], s_recv.at[kind, i], sibling)
+
+    def project(j):
+        def block(m):
+            total = jnp.dot(A[0, m], W[j, 0], preferred_element_type=jnp.float32)
+            for b_ in range(1, NB):
+                total = total + jnp.dot(A[b_, m], W[j, b_], preferred_element_type=jnp.float32)
+            return total
+
+        @pl.loop(0, 2)
+        def _(s_):
+            psend[j, s_] = block(2 * (1 - h) + s_).astype(jnp.bfloat16)
+
+        send(psend.at[j], precv.at[j], p_send.at[j], p_recv.at[j], h_far)
+
+        @pl.loop(0, 2)
+        def _(s_):
+            out[j, s_] = block(2 * h + s_)
+
+    peers = ((sibling, 0), (lo_pair, 1), (cross, 2))
+    for to, k in peers:
+        send(ssq.at[b], ssq.at[b], q_send.at[k], q_recv.at[k], to)
+    z_out(0)
+    z_out(1)
+    for to, k in peers:
+        arrive(ssq.at[(b // 2 * 2 + 1 - c) if k == 0 else (b_lo if k == 1 else (1 - lo) * 2 + 1 - c)],
+               q_send.at[k], q_recv.at[k], to)
+    total = ssq[0] + ssq[1] + ssq[2] + ssq[3]
+    width = NB * tokens.shape[1]
+    inverse = lax.rsqrt(jnp.sum(total, axis=1, keepdims=True) * (1.0 / width) + NORM_EPS)
+    gains = gain[...].astype(jnp.float32)
+    scaled = (tokens[...].astype(jnp.float32) * inverse * gains).astype(jnp.bfloat16)
+    N[0, s] = scaled[:, :depth]
+    N[1, s] = scaled[:, depth:]
+    tokens_out(0, s)
+    send(N.at[1 - h, s], N.at[1 - h, s], t_send.at[3, 0], t_recv.at[3, 0], z_pair)
+    send(N.at[h, s], N.at[h, s], t_send.at[3, 1], t_recv.at[3, 1], z_pair)
+    x_out(0)
+    z_out(2)
+    x_out(1)
+    x_on(0)
+    z_out(3)
+    tokens_on(0, s)
+    for k, h_ in ((0, 1 - h), (1, h)):
+        arrive(N.at[h_, 1 - s], t_send.at[3, k], t_recv.at[3, k], z_pair)
+    tokens_out(1, 1 - s)
+    x_out(2)
+    x_on(1)
+    z_out(4)
+    tokens_last(0, s)
+    x_out(3)
+    x_on(2)
+    z_out(5)
+    tokens_on(1, 1 - s)
+    x_out(4)
+    x_on(3)
+    z_out(6)
+    x_out(5)
+    x_on(4)
+    tokens_last(1, 1 - s)
+    x_out(6)
+    tokens_end()
+    for j in range(heads):
+        if j == 3:
+            x_on(5)
+        if j == 5:
+            x_on(6)
+        x_end(j)
+        project(j)
+    for j in range(heads):
+        arrive(precv.at[j], p_send.at[j], p_recv.at[j], h_far)
+        out[j] = out[j] + precv[j].astype(jnp.float32)
+    for copy in sent:
+        copy.wait_send()
+
+
+def project_tokens(narrow, tokens, gain):
+    twice, rows, lanes = narrow.shape
+    heads = twice // 2
+    count, width = tokens.shape
+    depth = width // 2
+    assert depth == NZ * rows
+    dma = pltpu.SemaphoreType.DMA
+    vmem = pl.BlockSpec(memory_space=pltpu.VMEM)
+    return pl.pallas_call(
+        projection_kernel,
+        name="gather_project",
+        out_shape=jax.ShapeDtypeStruct((heads, 2, count, lanes), jnp.float32),
+        in_specs=[vmem] * 3,
+        out_specs=vmem,
+        scratch_shapes=[
+            pltpu.VMEM((heads, NX, depth, lanes), jnp.bfloat16),
+            pltpu.VMEM((NB, 2 * NH, count, depth), jnp.bfloat16),
+            pltpu.VMEM((NH, 2, count, depth), jnp.bfloat16),
+            pltpu.VMEM((NB, count, lanes), jnp.float32),
+            pltpu.VMEM((heads, 2, count, lanes), jnp.bfloat16),
+            pltpu.VMEM((heads, 2, count, lanes), jnp.bfloat16),
+            dma((heads, NZ)), dma((heads, NZ)),
+            dma((heads, 6)), dma((heads, 6)),
+            dma((3,)), dma((3,)),
+            dma((5, 2)), dma((5, 2)),
+            dma((4, 2)), dma((4, 2)),
+            dma((heads,)), dma((heads,)),
+        ],
+        compiler_params=pltpu.CompilerParams(
+            collective_id=0, has_side_effects=True, vmem_limit_bytes=40 << 20
+        ),
+        cost_estimate=pl.CostEstimate(
+            flops=2 * 4 * count * 4 * depth * heads * lanes, bytes_accessed=4 << 20, transcendentals=0
+        ),
+    )(narrow, tokens, gain)
 
 
 def rotate(values, positions):
@@ -101,47 +347,36 @@
     new_master, new_first, new_second = adam_update(
         weight_master, gradient, first_moment, second_moment
     )
-    narrow = new_master.astype(jnp.bfloat16)
-    half_cols = narrow.shape[1] // 2
+    head_dim = key_cache.shape[-1]
+    rows_here, columns = new_master.shape
+    half_cols = columns // 2
+    per_group = half_cols // head_dim
+    narrow = new_master.astype(jnp.bfloat16).reshape(rows_here, 2 * per_group, head_dim)
+    narrow = narrow.transpose(1, 0, 2)
     fsdp_index = lax.axis_index("fsdp")
     parity = fsdp_index % 2
-    gathered = lax.all_gather(narrow, "fsdp", axis=0, tiled=True)
-    own_weight = lax.dynamic_slice_in_dim(gathered, parity * half_cols, half_cols, 1)
     own_bias = lax.dynamic_slice_in_dim(query_key_value_bias, parity * half_cols, half_cols, 0)
-    full_tokens, full_gain = (
-        lax.all_gather(new_tokens, "tp", axis=2, tiled=True),
-        lax.all_gather(norm_gain, "tp", axis=0, tiled=True),
-    )
-    other_tokens = partner(full_tokens, "fsdp", 0)
     is_first = parity == 0
-    group_tokens = jnp.concatenate(
-        [
-            jnp.where(is_first, full_tokens, other_tokens),
-            jnp.where(is_first, other_tokens, full_tokens),
-        ],
-        axis=1,
-    )
-    steps_here, group_rows, model_width = group_tokens.shape
+    steps_here, own_rows, features = new_tokens.shape
+    group_rows = 2 * own_rows
     group_start = fsdp_index // 2 * group_rows
     group_len = lax.dynamic_slice_in_dim(cache_len, group_start, group_rows, 0)
-    normed = rms_scale(group_tokens, full_gain)
-    joined_projection = jnp.dot(
-        normed.reshape(steps_here * group_rows, model_width),
-        own_weight,
-        preferred_element_type=jnp.float32,
-    )
-    joined_projection = joined_projection + own_bias.astype(jnp.float32)
-    head_dim = key_cache.shape[-1]
-    per_group = half_cols // head_dim
-    joined_projection = joined_projection.reshape(steps_here, group_rows, 1, per_group, head_dim)
+    joined = project_tokens(
+        narrow, new_tokens.reshape(steps_here * own_rows, features), norm_gain.reshape(1, features)
+    )
+    joined = joined + own_bias.astype(jnp.float32).reshape(per_group, 1, 1, head_dim)
+    joined = joined.reshape(per_group, 2, steps_here, own_rows, head_dim)
+    joined = joined.transpose(2, 1, 3, 0, 4).reshape(
+        steps_here, group_rows, 1, per_group, head_dim
+    )
     positions = group_len[None, :] + jnp.arange(steps_here, dtype=jnp.int32)[:, None]
     queries = rotate(
-        joined_projection[:, :, :, : per_group - 2], positions[:, :, None, None]
+        joined[:, :, :, : per_group - 2], positions[:, :, None, None]
     ).astype(jnp.bfloat16)
-    keys_new = rotate(joined_projection[:, :, :, per_group - 2], positions[:, :, None]).astype(
+    keys_new = rotate(joined[:, :, :, per_group - 2], positions[:, :, None]).astype(
         jnp.bfloat16
     )
-    values_new = joined_projection[:, :, :, per_group - 1].astype(jnp.bfloat16)
+    values_new = joined[:, :, :, per_group - 1].astype(jnp.bfloat16)
     attended = attend(queries, keys_new, values_new, key_cache[0], value_cache[0], group_len)
     attended = attended.reshape(steps_here, group_rows, (per_group - 2) * head_dim)
     own_count = group_rows // 2

time: 302 us -> 106 us (0.35)
  waiting for transfers between devices: 233 us -> 6.32 us
  Pallas kernels: 0 us -> 71.6 us
  between operations: 14.3 us -> 0.93 us
  matrix products: 18.7 us -> 8.98 us
  other arithmetic: 20 us -> 11.2 us
  blocking collectives: 5.19 us -> 0 us
    all_gather x2 -> x0, waiting for transfers between devices: 183 us -> none  [the longest x1 151 us: on_device(): gathered = lax.all_gather(narrow, 'fsdp', axis=0, tiled=True)]
    pallas_call x0 -> x1, Pallas kernels: none -> 71.6 us  [project_tokens(): pl.pallas_call(projection_kernel, name='gather_project', out_shape=jax.Sh...]
    ppermute x2 -> x1, waiting for transfers between devices: 49.7 us -> 6.32 us  [partner(): return lax.ppermute(block, axis, route)]
    dot_general x1 -> x0, matrix products: 9.67 us -> none  [on_device(): jnp.dot(normed.reshape(steps_here * group_rows, model_width), own_weight,...]
    convert_element_type x5 -> x0, other arithmetic: 9.03 us -> none  [the longest x1 3.26 us: rms_scale(): (floats * inverse * gain_row.astype(jnp.float32)).astype(jnp.bfloat16)]
    all_gather x1 -> x0, blocking collectives: 5.19 us -> none  [on_device(): lax.all_gather(norm_gain, 'tp', axis=0, tiled=True)]
  transfers between devices with their start and end apart: 4 -> 1, of which waited for: 4 -> 1; matrix products, arithmetic and copies ran while one was open for 5% -> 0% of each run, Pallas kernels for 0% -> 0%
where the time goes in v1:
time: 106 us; the launch traced here: 105 us
  Pallas kernels  71.6 us (68%)
  other arithmetic  11.2 us (11%)
  matrix products  8.98 us (8%)
  waiting for transfers between devices  6.32 us (6%)
  local copies, waits for them, and re-layouts  4.83 us (5%)
    pallas_call x1, Pallas kernels, project_tokens(): pl.pallas_call(projection_kernel, name='gather_project', out_shape=jax.Sh...  71.6 us
    ppermute x1, waiting for transfers between devices, partner(): return lax.ppermute(block, axis, route)  6.32 us
    dot_general x1, matrix products, attend(): jnp.einsum('srbph,trbh->srbpt', queries, keys_new, preferred_element_type...  3.77 us
    unnamed x1, other arithmetic  3.01 us
    concatenate x2, other arithmetic, rotate(): jnp.concatenate([first_part * cosine - second_part * sine_part, second_pa...  2.66 us
    dot_general x1, matrix products, attend(): jnp.einsum('srbph,brlh->srbpl', queries, cached_keys, preferred_element_t...  2.59 us
    reduce_sum x2, other arithmetic, attend(): row_total = jnp.sum(cached_exp, axis=-1) + jnp.sum(fresh_exp, axis=-1)  2.23 us
  transfers between devices with their start and end apart: 1, of which 1 were waited for; matrix products, arithmetic and copies ran while one was open for 0% of the time, Pallas kernels for 0%

profile of v1, /device:TPU:32, one launch (start us, length us, event | category | flops | bytes accessed | tf_op | source)
XLA Modules:
  0.0 104.9 jit_solution(2389958947788496491)
XLA Ops:
  0.6 0.0 copy-start.2
  0.6 0.0 copy-start
  0.7 0.8 dynamic_slice.12
  1.6 0.1 iota_compare_fusion
  1.6 0.1 add_convert_fusion.1
  1.7 0.7 reshape.246.gain
  2.4 3.0 %convert_bitcast_fusion = (bf16[10,14,8,128]{3,2,1,0:T(8,128)(2,1)S(1)}, f32[80,1792]{1,0:T(8,128)}, f32[80,1792]{1,0:T(8,128)}, f32[80,1792]{1,0:T(8,128)}) fusion(f32[80,1792]{1,0:T(8,128)} %param.10, f32[80,1792]{1,0:T(8,128)} %param.11, f32[80,1792]{1,0:T(8,128)} %param.12, f32[80,1792]{1,0:T(8,128)} %param.13), kind=kLoop, calls=%fused_computation.40 | loop fusion | flops 2007040 | bytes 4300800
  5.4 0.1 copy.44
  5.5 0.0 copy-done.2
  5.5 0.1 bitcast_convert_fusion
  5.6 0.0 copy-done
  5.6 71.6 %gather_project.1 = f32[7,2,192,128]{3,2,1,0:T(8,128)S(1)} custom-call(bf16[14,80,128]{2,1,0:T(8,128)(2,1)S(1)} %bitcast.102, bf16[192,1280]{1,0:T(8,128)(2,1)S(1)} %bitcast.103, bf16[1,1280]{1,0:T(2,128)(2,1)S(1)} %reshape.246.gain), custom_call_target="tpu_custom_call" | custom-call | flops 3523215360 | bytes 4194304 | tf_op jit(solution)/shard_map/gather_project/pallas_call | solution.py:256
  77.2 0.1 broadcast_add_fusion
  77.3 0.8 copy.24
  78.1 0.2 slice.30
  78.3 0.2 slice.59
  78.6 0.0 copy-start.1
  78.6 1.6 %multiply_cosine_fusion.1 = (f32[4,96,64]{2,0,1:T(4,128)S(1)}, f32[4,96,64]{2,0,1:T(4,128)S(1)}) fusion(f32[64]{0:T(128)S(1)} %multiply_power_fusion, f32[4,96]{0,1:T(8,128)S(1)} %add_convert_fusion.1), kind=kLoop, calls=%fused_computation.44 | loop fusion | flops 24576 | bytes 198400 | tf_op jit(solution)/shard_map/cos | solution.py:291
  80.2 2.0 %fusion.34 = (bf16[4,96,64]{2,0,1:T(4,128)(2,1)S(1)}, bf16[4,96,64]{2,0,1:T(4,128)(2,1)S(1)}) fusion(f32[4,96,1,128]{3,0,1,2:T(4,128)S(1)} %bitcast.110, f32[64]{0:T(128)S(1)} %multiply_power_fusion, f32[4,96]{0,1:T(8,128)S(1)} %add_convert_fusion.1), kind=kLoop, calls=%fused_computation.61 | loop fusion | flops 221184 | bytes 296704 | tf_op jit(solution)/shard_map/concatenate | solution.py:295
  82.2 0.7 fusion.16
  82.9 0.0 copy-done.1
  82.9 2.6 %fusion.6 = (f32[4,96,5]{2,0,1:T(4,128)S(1)}, f32[96,4,5,160]{3,2,1,0:T(8,128)S(1)}) fusion(pred[96,160]{1,0:T(8,128)(4,1)S(1)} %iota_compare_fusion, bf16[1,1,96,160,128]{4,3,2,1,0:T(8,128)(2,1)S(1)} %copy-done.1, bf16[4,96,5,64]{3,2,0,1:T(8,128)(2,1)S(1)} %get-tuple-element.13, bf16[4,96,5,64]{3,2,0,1:T(8,128)(2,1)S(1)} %get-tuple-element.12), kind=kOutput, calls=%fused_computation.9 | convolution fusion | flops 80545920 | bytes 5675520 | tf_op jit(solution)/shard_map/srbph,brlh->srbpl/dot_general | solution.py:307
  85.5 3.8 %fusion.40 = (f32[4,96,5]{2,0,1:T(4,128)S(1)}, f32[4,96,1,5,4]{3,4,0,1,2:T(4,128)S(1)}) fusion(bf16[4,96,5,64]{3,2,0,1:T(8,128)(2,1)S(1)} %get-tuple-element.13, bf16[4,96,5,64]{3,2,0,1:T(8,128)(2,1)S(1)} %get-tuple-element.12, bf16[4,96,64]{2,0,1:T(4,128)(2,1)S(1)} %get-tuple-element.17, bf16[4,96,64]{2,0,1:T(4,128)(2,1)S(1)} %get-tuple-element.16, ...), kind=kOutput, calls=%fused_computation.71 | convolution fusion | flops 3166848 | bytes 628240 | tf_op jit(solution)/shard_map/srbph,trbh->srbpt/dot_general | solution.py:314
  89.3 0.0 copy-start.3
  89.3 0.1 max.9
  89.4 0.7 fusion.18
  90.1 1.5 %fusion.5 = f32[4,96,5]{2,0,1:T(4,128)S(1)} fusion(f32[96,4,5,160]{3,2,1,0:T(8,128)S(1)} %get-tuple-element.21, f32[4,96,5]{2,0,1:T(4,128)S(1)} %max.9, pred[96,160]{1,0:T(8,128)(4,1)S(1)} %iota_compare_fusion), kind=kLoop, calls=%fused_computation.8 | loop fusion | flops 1226880 | bytes 1259520 | tf_op jit(solution)/shard_map/reduce_sum | solution.py:323
  91.6 0.1 add.101
  91.7 0.0 copy-done.3
  91.7 2.0 %fusion = f32[96,4,5,128]{3,2,1,0:T(8,128)S(1)} fusion(bf16[1,1,96,160,128]{4,3,2,1,0:T(8,128)(2,1)S(1)} %copy-done.3, f32[96,4,5,160]{3,2,1,0:T(8,128)S(1)} %get-tuple-element.21, f32[4,96,5]{2,0,1:T(4,128)S(1)} %add.101, f32[4,96,5]{2,0,1:T(4,128)S(1)} %max.9, pred[96,160]{1,0:T(8,128)(4,1)S(1)} %iota_compare_fusion), kind=kOutput, calls=%fused_computation | convolution fusion | flops 80179200 | bytes 6174720 | tf_op jit(solution)/shard_map/srbpl,brlh->srbph/dot_general | solution.py:326
  93.6 0.7 fusion.14
  94.3 0.7 copy.27
  95.0 0.2 constant_dynamic-slice_fusion
  95.3 0.2 copy.28
  95.5 1.0 collective-permute-start
  96.5 6.3 %collective-permute-done = bf16[4,48,640]{2,1,0:T(8,128)(2,1)S(1)} collective-permute-done((bf16[4,48,640]{2,1,0:T(8,128)(2,1)S(1)}, bf16[4,48,640]{2,1,0:T(8,128)(2,1)S(1)}, u32[]{:S(2)}, u32[]{:S(2)}) %collective-permute-start) | collective-permute-done | bytes 245792 | tf_op jit(solution)/shard_map/ppermute | solution.py:29
  102.8 0.3 copy.29
  103.1 0.4 broadcast_select_fusion.1
  103.5 0.2 copy.31
  103.8 0.2 copy.32
  104.0 0.8 pad_maximum_fusion.1
  (3 shorter events, 0.0 us)
Async XLA Ops:
  0.6 4.9 %copy-start.2 = (bf16[1792]{0:T(1024)(128)(2,1)S(1)}, bf16[1792]{0:T(1024)(128)(2,1)}, u32[]{:S(2)}) copy-start(bf16[1792]{0:T(1024)(128)(2,1)} %param.14) | copy-start | bytes 10756
  0.6 5.0 %copy-start = (bf16[4,48,1280]{2,1,0:T(8,128)(2,1)S(1)}, bf16[4,48,1280]{2,1,0:T(8,128)(2,1)}, u32[]{:S(2)}) copy-start(bf16[4,48,1280]{2,1,0:T(8,128)(2,1)} %param.15) | copy-start | bytes 1474564
  78.6 4.4 %copy-start.1 = (bf16[1,1,96,160,128]{4,3,2,1,0:T(8,128)(2,1)S(1)}, bf16[1,1,96,160,128]{4,3,2,1,0:T(8,128)(2,1)}, u32[]{:S(2)}) copy-start(bf16[1,1,96,160,128]{4,3,2,1,0:T(8,128)(2,1)} %param.18) | copy-start | bytes 11796484
  89.3 2.4 %copy-start.3 = (bf16[1,1,96,160,128]{4,3,2,1,0:T(8,128)(2,1)S(1)}, bf16[1,1,96,160,128]{4,3,2,1,0:T(8,128)(2,1)}, u32[]{:S(2)}) copy-start(bf16[1,1,96,160,128]{4,3,2,1,0:T(8,128)(2,1)} %param.19) | copy-start | bytes 11796484
  95.5 7.3 %collective-permute-start = (bf16[4,48,640]{2,1,0:T(8,128)(2,1)S(1)}, bf16[4,48,640]{2,1,0:T(8,128)(2,1)S(1)}, u32[]{:S(2)}, u32[]{:S(2)}) collective-permute-start(bf16[4,48,640]{2,1,0:T(8,128)(2,1)S(1)} %copy.28), channel_id=1, source_target_pairs={{0,4},{4,0},{8,12},{12,8},{16,20},{20,16},{24,28},{28,24},{32,36},... | collective-permute-start | bytes 737288 | tf_op jit(solution)/shard_map/ppermute | solution.py:29

commit v2 on v1

--- a/solution.py
+++ b/solution.py
@@ -1,5 +1,8 @@
+import math
+
 import jax
 import jax.numpy as jnp
+import numpy as np
 from jax import lax
 from jax.experimental import pallas as pl
 from jax.experimental.pallas import tpu as pltpu
@@ -17,16 +20,8 @@
 MESH = pl.DeviceIdType.MESH
 NX, NH, NZ = 4, 2, 8
 NB = 4
-
-
-def partner(block, axis, stride):
-    count = lax.axis_size(axis)
-    route = []
-    for low in range(count):
-        high = low | 1 << stride
-        if high != low and high < count:
-            route += [(low, high), (high, low)]
-    return lax.ppermute(block, axis, route)
+NEW = 4
+AT_ONCE = 4
 
 
 def adam_update(weight_master, gradient, first_moment, second_moment):
@@ -36,10 +31,11 @@
     return (weight_master - LEARN_RATE * step_size, new_first, new_second)
 
 
-def projection_kernel(
-    narrow, tokens, gain, out, W, A, N, ssq, psend, precv,
+def layer_kernel(
+    lengths, frequency, narrow, tokens, gain, bias, keys_in, values_in, context,
+    W, A, N, ssq, psend, precv, J, cosine, sine, keys, values, mine, theirs,
     z_send, z_recv, x_send, x_recv, q_send, q_recv,
-    t_send, t_recv, s_send, s_recv, p_send, p_recv,
+    t_send, t_recv, s_send, s_recv, p_send, p_recv, e_send, e_recv, c_sem,
 ):
     heads, _, depth, lanes = W.shape
     rows = depth // NZ
@@ -68,7 +64,20 @@
     for other in everyone:
         pl.semaphore_signal(barrier, inc=1, device_id=other, device_id_type=MESH)
 
-    flat = tokens[...].astype(jnp.float32)
+    loads = [
+        pltpu.make_async_copy(keys_in, keys, c_sem.at[0]),
+        pltpu.make_async_copy(values_in, values, c_sem.at[1]),
+    ]
+    for load in loads:
+        load.start()
+
+    count, width = tokens.shape
+    own_rows = count // NEW
+    to_row = lax.broadcasted_iota(jnp.int32, (count, count), 0)
+    to_col = lax.broadcasted_iota(jnp.int32, (count, count), 1)
+    order = (to_col == to_row % NEW * own_rows + to_row // NEW).astype(jnp.bfloat16)
+    back = (to_row == to_col % NEW * own_rows + to_col // NEW).astype(jnp.bfloat16)
+    flat = jnp.dot(order, tokens[...], preferred_element_type=jnp.float32)
     square = flat * flat
     part = square[:, :lanes]
     for k in range(1, square.shape[1] // lanes):
@@ -186,7 +195,22 @@
 
         @pl.loop(0, 2)
         def _(s_):
-            out[j, s_] = block(2 * h + s_)
+            J[j, s_] = block(2 * h + s_)
+
+    own_lens = f // 2 * (2 * own_rows)
+    two_rows = 2 * NEW
+    down = lax.broadcasted_iota(jnp.int32, (two_rows, 1), 0)
+    sign = jnp.where(lax.broadcasted_iota(jnp.int32, (1, lanes), 1) < lanes // 2, -1.0, 1.0)
+
+    def tables(s_):
+        @pl.loop(0, own_rows // 2)
+        def _(i):
+            r = own_lens + s_ * own_rows + 2 * i
+            position = jnp.where(down < NEW, lengths[r], lengths[r + 1]) + down % NEW
+            angle = position.astype(jnp.float32) * frequency[...]
+            here = pl.ds(pl.multiple_of(i * two_rows, two_rows), two_rows)
+            cosine[s_, here] = jnp.cos(angle)
+            sine[s_, here] = jnp.sin(angle) * sign
 
     peers = ((sibling, 0), (lo_pair, 1), (cross, 2))
     for to, k in peers:
@@ -197,10 +221,9 @@
         arrive(ssq.at[(b // 2 * 2 + 1 - c) if k == 0 else (b_lo if k == 1 else (1 - lo) * 2 + 1 - c)],
                q_send.at[k], q_recv.at[k], to)
     total = ssq[0] + ssq[1] + ssq[2] + ssq[3]
-    width = NB * tokens.shape[1]
-    inverse = lax.rsqrt(jnp.sum(total, axis=1, keepdims=True) * (1.0 / width) + NORM_EPS)
-    gains = gain[...].astype(jnp.float32)
-    scaled = (tokens[...].astype(jnp.float32) * inverse * gains).astype(jnp.bfloat16)
+    inverse = lax.rsqrt(jnp.sum(total, axis=1, keepdims=True) * (1.0 / (NB * width)) + NORM_EPS)
+    gains = gain[...].astype(jnp.float32).reshape(1, width)
+    scaled = (flat * inverse * gains).astype(jnp.bfloat16)
     N[0, s] = scaled[:, :depth]
     N[1, s] = scaled[:, depth:]
     tokens_out(0, s)
@@ -216,10 +239,12 @@
         arrive(N.at[h_, 1 - s], t_send.at[3, k], t_recv.at[3, k], z_pair)
     tokens_out(1, 1 - s)
     x_out(2)
+    tables(0)
     x_on(1)
     z_out(4)
     tokens_last(0, s)
     x_out(3)
+    tables(1)
     x_on(2)
     z_out(5)
     tokens_on(1, 1 - s)
@@ -238,26 +263,108 @@
             x_on(6)
         x_end(j)
         project(j)
+    lens_at = f // 2 * (2 * own_rows)
+    queries = heads - 2
+    offsets = bias[...].astype(jnp.float32).reshape(1, 2 * heads * lanes)
+    offsets = jnp.where(s == 0, offsets[:, : heads * lanes], offsets[:, heads * lanes :])
     for j in range(heads):
         arrive(precv.at[j], p_send.at[j], p_recv.at[j], h_far)
-        out[j] = out[j] + precv[j].astype(jnp.float32)
+        offset = offsets[:, j * lanes : (j + 1) * lanes]
+        for s_ in (0, 1):
+            full = J[j, s_] + precv[j, s_].astype(jnp.float32) + offset
+            if j <= queries:
+                full = full * cosine[s_] + pltpu.roll(full, lanes // 2, 1) * sine[s_]
+            J[j, s_] = full.astype(jnp.bfloat16).astype(jnp.float32)
+
+    for load in loads:
+        load.wait()
+    slots = keys.shape[1]
+    two = 2 * NEW
+    wide = -(-(2 * slots + two) // 128) * 128
+    col = lax.broadcasted_iota(jnp.int32, (two, wide), 1)
+    row = lax.broadcasted_iota(jnp.int32, (two, wide), 0)
+    never = 1 << 20
+    second = (col >= slots).astype(jnp.int32)
+    place = jnp.where(second == row // NEW, col - second * slots, never)
+    new = col - 2 * slots
+    seen = (new // NEW == row // NEW) & (new % NEW <= row % NEW) & (new < two)
+    place = jnp.where(col < 2 * slots, place, jnp.where(seen, -1, never))
+    first_row = lax.broadcasted_iota(jnp.int32, (two, 1), 0) < NEW
+    scale = 1.0 / math.sqrt(lanes)
+
+    def extend(cached, fresh):
+        rest = jnp.zeros((wide - 2 * slots - two, lanes), jnp.float32)
+        tail = jnp.concatenate([fresh, rest], axis=0).astype(jnp.bfloat16)
+        return jnp.concatenate([cached.reshape(2 * slots, lanes), tail], axis=0)
+
+    def pair(s_, i):
+        rows_here = pl.ds(pl.multiple_of(i * two, two), two)
+        r = s_ * own_rows + 2 * i
+        q = jnp.concatenate([J[j, s_, rows_here] for j in range(queries)], axis=0)
+        k = extend(keys[pl.ds(r, 2)], J[queries, s_, rows_here])
+        scores = lax.dot_general(
+            q.astype(jnp.bfloat16), k, (((1,), (1,)), ((), ())),
+            preferred_element_type=jnp.float32,
+        ) * scale
+        limit = jnp.where(first_row, lengths[lens_at + r], lengths[lens_at + r + 1])
+        scores = scores.reshape(queries, two, wide)
+        scores = jnp.where((place < limit)[None], scores, -jnp.inf)
+        grown = jnp.exp(scores - jnp.max(scores, axis=-1, keepdims=True))
+        probs = grown * (1.0 / jnp.sum(grown, axis=-1, keepdims=True))
+        probs = probs.reshape(queries * two, wide).astype(jnp.bfloat16)
+        v = extend(values[pl.ds(r, 2)], J[queries + 1, s_, rows_here])
+        return jnp.dot(probs, v, preferred_element_type=jnp.float32)
+
+    block_rows = AT_ONCE * two
+
+    def attend(s_, blocks, into):
+        @pl.loop(*blocks)
+        def _(t):
+            done = [pair(s_, t * AT_ONCE + k) for k in range(AT_ONCE)]
+            for j in range(queries):
+                tile = jnp.concatenate([d[j * two : (j + 1) * two] for d in done], axis=0)
+                into[pl.ds(pl.multiple_of(t * block_rows, 16), block_rows),
+                     j * lanes : (j + 1) * lanes] = tile.astype(jnp.bfloat16)
+
+    blocks = count // block_rows
+    cut = blocks // 2
+    for k, (start, stop) in enumerate(((0, cut), (cut, blocks))):
+        attend(1 - s, (start, stop), mine.at[0])
+        span = pl.ds(start * block_rows, (stop - start) * block_rows)
+        send(mine.at[0, span], theirs.at[span], e_send.at[k], e_recv.at[k], z_pair)
+    attend(s, (0, blocks), mine.at[1])
+    piece = queries * lanes
+    context[:, pl.ds(pl.multiple_of(s * piece, 128), piece)] = jnp.dot(
+        back, mine[1], preferred_element_type=jnp.float32
+    ).astype(jnp.bfloat16)
+    for k, (start, stop) in enumerate(((0, cut), (cut, blocks))):
+        span = pl.ds(start * block_rows, (stop - start) * block_rows)
+        arrive(theirs.at[span], e_send.at[k], e_recv.at[k], z_pair)
+    context[:, pl.ds(pl.multiple_of((1 - s) * piece, 128), piece)] = jnp.dot(
+        back, theirs[...], preferred_element_type=jnp.float32
+    ).astype(jnp.bfloat16)
     for copy in sent:
         copy.wait_send()
 
 
-def project_tokens(narrow, tokens, gain):
+def project_tokens(lengths, narrow, tokens, gain, bias, keys, values):
     twice, rows, lanes = narrow.shape
     heads = twice // 2
     count, width = tokens.shape
     depth = width // 2
     assert depth == NZ * rows
+    piece = (heads - 2) * lanes
+    half_lanes = lanes // 2
+    frequency = ROPE_BASE ** (-(np.arange(lanes) % half_lanes) / half_lanes)
+    frequency = jnp.asarray(frequency.reshape(1, lanes), jnp.float32)
     dma = pltpu.SemaphoreType.DMA
     vmem = pl.BlockSpec(memory_space=pltpu.VMEM)
+    hbm = pl.BlockSpec(memory_space=pl.ANY)
     return pl.pallas_call(
-        projection_kernel,
+        layer_kernel,
         name="gather_project",
-        out_shape=jax.ShapeDtypeStruct((heads, 2, count, lanes), jnp.float32),
-        in_specs=[vmem] * 3,
+        out_shape=jax.ShapeDtypeStruct((count, 2 * piece), jnp.bfloat16),
+        in_specs=[pl.BlockSpec(memory_space=pltpu.SMEM)] + [vmem] * 5 + [hbm] * 2,
         out_specs=vmem,
         scratch_shapes=[
             pltpu.VMEM((heads, NX, depth, lanes), jnp.bfloat16),
@@ -266,70 +373,28 @@
             pltpu.VMEM((NB, count, lanes), jnp.float32),
             pltpu.VMEM((heads, 2, count, lanes), jnp.bfloat16),
             pltpu.VMEM((heads, 2, count, lanes), jnp.bfloat16),
+            pltpu.VMEM((heads, 2, count, lanes), jnp.float32),
+            pltpu.VMEM((2, count, lanes), jnp.float32),
+            pltpu.VMEM((2, count, lanes), jnp.float32),
+            pltpu.VMEM(keys.shape, keys.dtype),
+            pltpu.VMEM(values.shape, values.dtype),
+            pltpu.VMEM((2, count, piece), jnp.bfloat16),
+            pltpu.VMEM((count, piece), jnp.bfloat16),
             dma((heads, NZ)), dma((heads, NZ)),
             dma((heads, 6)), dma((heads, 6)),
             dma((3,)), dma((3,)),
             dma((5, 2)), dma((5, 2)),
             dma((4, 2)), dma((4, 2)),
             dma((heads,)), dma((heads,)),
+            dma((2,)), dma((2,)), dma((2,)),
         ],
         compiler_params=pltpu.CompilerParams(
-            collective_id=0, has_side_effects=True, vmem_limit_bytes=40 << 20
+            collective_id=0, has_side_effects=True, vmem_limit_bytes=48 << 20
         ),
         cost_estimate=pl.CostEstimate(
-            flops=2 * 4 * count * 4 * depth * heads * lanes, bytes_accessed=4 << 20, transcendentals=0
+            flops=2 * 4 * count * 4 * depth * heads * lanes, bytes_accessed=12 << 20, transcendentals=0
         ),
-    )(narrow, tokens, gain)
-
-
-def rotate(values, positions):
-    half_width = values.shape[-1] // 2
-    inverse = jnp.power(
-        ROPE_BASE, -jnp.arange(half_width, dtype=jnp.float32) * (2.0 / (2 * half_width))
-    )
-    angles = positions.astype(jnp.float32)[..., None] * inverse
-    cosine = jnp.cos(angles)
-    sine_part = jnp.sin(angles)
-    first_part = values[..., :half_width]
-    second_part = values[..., half_width:]
-    return jnp.concatenate(
-        [
-            first_part * cosine - second_part * sine_part,
-            second_part * cosine + first_part * sine_part,
-        ],
-        axis=-1,
-    )
-
-
-def attend(queries, keys_new, values_new, cached_keys, cached_values, lengths):
-    score_scale = 1.0 / jnp.sqrt(jnp.float32(queries.shape[-1]))
-    cached_scores = (
-        jnp.einsum("srbph,brlh->srbpl", queries, cached_keys, preferred_element_type=jnp.float32)
-        * score_scale
-    )
-    position = jnp.arange(cached_keys.shape[2], dtype=jnp.int32)
-    valid_mask = position[None, :] < lengths[:, None]
-    cached_scores = jnp.where(valid_mask[None, :, None, None, :], cached_scores, -jnp.inf)
-    fresh_scores = (
-        jnp.einsum("srbph,trbh->srbpt", queries, keys_new, preferred_element_type=jnp.float32)
-        * score_scale
-    )
-    steps_here = queries.shape[0]
-    causal = jnp.arange(steps_here)[:, None] >= jnp.arange(steps_here)[None, :]
-    fresh_scores = jnp.where(causal[:, None, None, None, :], fresh_scores, -jnp.inf)
-    row_max = jnp.maximum(jnp.max(cached_scores, axis=-1), jnp.max(fresh_scores, axis=-1))
-    cached_exp = jnp.exp(cached_scores - row_max[..., None])
-    fresh_exp = jnp.exp(fresh_scores - row_max[..., None])
-    row_total = jnp.sum(cached_exp, axis=-1) + jnp.sum(fresh_exp, axis=-1)
-    cached_prob = (cached_exp / row_total[..., None]).astype(jnp.bfloat16)
-    fresh_prob = (fresh_exp / row_total[..., None]).astype(jnp.bfloat16)
-    mixed = jnp.einsum(
-        "srbpl,brlh->srbph", cached_prob, cached_values, preferred_element_type=jnp.float32
-    )
-    mixed = mixed + jnp.einsum(
-        "srbpt,trbh->srbph", fresh_prob, values_new, preferred_element_type=jnp.float32
-    )
-    return mixed.astype(jnp.bfloat16)
+    )(lengths, frequency, narrow, tokens, gain, bias, keys, values)
 
 
 def on_device(
@@ -353,40 +418,12 @@
     per_group = half_cols // head_dim
     narrow = new_master.astype(jnp.bfloat16).reshape(rows_here, 2 * per_group, head_dim)
     narrow = narrow.transpose(1, 0, 2)
-    fsdp_index = lax.axis_index("fsdp")
-    parity = fsdp_index % 2
-    own_bias = lax.dynamic_slice_in_dim(query_key_value_bias, parity * half_cols, half_cols, 0)
-    is_first = parity == 0
     steps_here, own_rows, features = new_tokens.shape
-    group_rows = 2 * own_rows
-    group_start = fsdp_index // 2 * group_rows
-    group_len = lax.dynamic_slice_in_dim(cache_len, group_start, group_rows, 0)
-    joined = project_tokens(
-        narrow, new_tokens.reshape(steps_here * own_rows, features), norm_gain.reshape(1, features)
+    output = project_tokens(
+        cache_len, narrow, new_tokens.reshape(steps_here * own_rows, features), norm_gain,
+        query_key_value_bias, key_cache[0, 0], value_cache[0, 0],
     )
-    joined = joined + own_bias.astype(jnp.float32).reshape(per_group, 1, 1, head_dim)
-    joined = joined.reshape(per_group, 2, steps_here, own_rows, head_dim)
-    joined = joined.transpose(2, 1, 3, 0, 4).reshape(
-        steps_here, group_rows, 1, per_group, head_dim
-    )
-    positions = group_len[None, :] + jnp.arange(steps_here, dtype=jnp.int32)[:, None]
-    queries = rotate(
-        joined[:, :, :, : per_group - 2], positions[:, :, None, None]
-    ).astype(jnp.bfloat16)
-    keys_new = rotate(joined[:, :, :, per_group - 2], positions[:, :, None]).astype(
-        jnp.bfloat16
-    )
-    values_new = joined[:, :, :, per_group - 1].astype(jnp.bfloat16)
-    attended = attend(queries, keys_new, values_new, key_cache[0], value_cache[0], group_len)
-    attended = attended.reshape(steps_here, group_rows, (per_group - 2) * head_dim)
-    own_count = group_rows // 2
-    own_context = lax.dynamic_slice_in_dim(attended, parity * own_count, own_count, 1)
-    their_context = lax.dynamic_slice_in_dim(attended, (1 - parity) * own_count, own_count, 1)
-    returned = partner(their_context, "fsdp", 0)
-    output = jnp.concatenate(
-        [jnp.where(is_first, own_context, returned), jnp.where(is_first, returned, own_context)],
-        axis=2,
-    )
+    output = output.reshape(steps_here, own_rows, features)
     return (new_master, new_first, new_second, output)
 
 

time: 106 us -> 96.3 us (0.908)
  Pallas kernels: 71.6 us -> 90.1 us
  matrix products: 8.98 us -> 0 us
  other arithmetic: 11.2 us -> 3.16 us
  waiting for transfers between devices: 6.32 us -> 0 us
  local copies, waits for them, and re-layouts: 4.83 us -> 0.86 us
    pallas_call x1, Pallas kernels: 71.6 us -> 90.1 us  [project_tokens(): pl.pallas_call(layer_kernel, name='gather_project', out_shape=jax.ShapeDt...]
    dot_general x4 -> x0, matrix products: 8.98 us -> none  [the longest x1 3.77 us: attend(): jnp.einsum('srbph,trbh->srbpt', queries, keys_new, preferred_element_type...]
    ppermute x1 -> x0, waiting for transfers between devices: 6.32 us -> none  [partner(): return lax.ppermute(block, axis, route)]
    concatenate x3 -> x0, other arithmetic: 3.48 us -> none  [the longest x2 2.66 us: rotate(): jnp.concatenate([first_part * cosine - second_part * sine_part, second_pa...]
    reduce_sum x2 -> x0, other arithmetic: 2.23 us -> none  [attend(): row_total = jnp.sum(cached_exp, axis=-1) + jnp.sum(fresh_exp, axis=-1)]
    cos x1 -> x0, other arithmetic: 1.64 us -> none  [rotate(): cosine = jnp.cos(angles)]
    dynamic_slice x3 -> x0, local copies, waits for them, and re-layouts: 1.31 us -> none  [the longest x1 0.83 us: on_device(): group_len = lax.dynamic_slice_in_dim(cache_len, group_start, group_rows, 0)]
  transfers between devices with their start and end apart: 1 -> 0, of which waited for: 1 -> 0; matrix products, arithmetic and copies ran while one was open for 0% -> 0% of each run, Pallas kernels for 0% -> 0%
where the time goes in v2:
time: 96.3 us; the launch traced here: 94.9 us
  Pallas kernels  90.1 us (94%)
  other arithmetic  3.16 us (3%)
    pallas_call x1, Pallas kernels, project_tokens(): pl.pallas_call(layer_kernel, name='gather_project', out_shape=jax.ShapeDt...  90.1 us
    unnamed x1, other arithmetic  3.16 us

profile of v2, /device:TPU:32, one launch (start us, length us, event | category | flops | bytes accessed | tf_op | source)
XLA Modules:
  0.0 94.9 jit_solution(12166323516266880303)
XLA Ops:
  0.6 0.0 copy-start.5
  0.6 0.0 copy-start
  0.7 0.0 copy-start.2
  0.7 0.0 copy-start.3
  0.7 0.0 copy-start.1
  0.7 0.0 copy-start.4
  0.7 3.2 %convert_bitcast_fusion = (bf16[10,14,8,128]{3,2,1,0:T(8,128)(2,1)S(1)}, f32[80,1792]{1,0:T(8,128)}, f32[80,1792]{1,0:T(8,128)}, f32[80,1792]{1,0:T(8,128)}) fusion(f32[80,1792]{1,0:T(8,128)} %param.11, f32[80,1792]{1,0:T(8,128)} %param.12, f32[80,1792]{1,0:T(8,128)} %param.13, f32[80,1792]{1,0:T(8,128)} %param.14), kind=kLoop, calls=%fused_computation.5 | loop fusion | flops 2007040 | bytes 4300800
  3.9 0.1 copy.18
  3.9 0.0 copy-done.5
  3.9 0.0 copy-done
  3.9 0.0 copy-done.2
  3.9 0.0 copy-done.3
  4.0 0.0 copy-done.1
  4.0 0.0 copy-done.4
  4.0 90.1 %gather_project.1 = bf16[192,1280]{1,0:T(8,128)(2,1)S(1)} custom-call(s32[3072]{0:T(1024)S(1)} %copy-done.2, f32[1,128]{1,0:T(1,128)S(1)} %copy-done.5, bf16[14,80,128]{2,1,0:T(8,128)(2,1)S(1)} %bitcast.13, bf16[192,1280]{1,0:T(8,128)(2,1)S(1)} %bitcast.15, bf16[1280]{0:T(1024)(128)(2,1)S(1)} %copy-done.3, bf16[1792]{0:T(1024)(128)(2,1)S(1)} %copy-done.4, ...), custom_call_target="tpu_custom_call" | custom-call | flops 3523215360 | bytes 12582912 | tf_op jit(solution)/shard_map/gather_project/pallas_call | solution.py:363
  94.1 0.8 copy.20
Async XLA Ops:
  0.6 3.3 %copy-start.5 = (f32[1,128]{1,0:T(1,128)S(1)}, f32[1,128]{1,0:T(1,128)}, u32[]{:S(2)}) copy-start(f32[1,128]{1,0:T(1,128)} %constant.20.clone.frequency) | copy-start | bytes 1540
  0.6 3.3 %copy-start = (bf16[1,1,96,160,128]{4,3,2,1,0:T(8,128)(2,1)S(1)}, bf16[1,1,96,160,128]{4,3,2,1,0:T(8,128)(2,1)}, u32[]{:S(2)}) copy-start(bf16[1,1,96,160,128]{4,3,2,1,0:T(8,128)(2,1)} %param.19) | copy-start | bytes 11796484
  0.7 3.3 %copy-start.2 = (s32[3072]{0:T(1024)S(1)}, s32[3072]{0:T(1024)}, u32[]{:S(2)}) copy-start(s32[3072]{0:T(1024)} %lengths.1) | copy-start | bytes 36868
  0.7 3.3 %copy-start.3 = (bf16[1280]{0:T(1024)(128)(2,1)S(1)}, bf16[1280]{0:T(1024)(128)(2,1)}, u32[]{:S(2)}) copy-start(bf16[1280]{0:T(1024)(128)(2,1)} %gain.1) | copy-start | bytes 7684
  0.7 3.3 %copy-start.1 = (bf16[4,48,1280]{2,1,0:T(8,128)(2,1)S(1)}, bf16[4,48,1280]{2,1,0:T(8,128)(2,1)}, u32[]{:S(2)}) copy-start(bf16[4,48,1280]{2,1,0:T(8,128)(2,1)} %param.16) | copy-start | bytes 1474564
  0.7 3.3 %copy-start.4 = (bf16[1792]{0:T(1024)(128)(2,1)S(1)}, bf16[1792]{0:T(1024)(128)(2,1)}, u32[]{:S(2)}) copy-start(bf16[1792]{0:T(1024)(128)(2,1)} %bias.1) | copy-start | bytes 10756

commit v3 on v2

--- a/solution.py
+++ b/solution.py
@@ -21,7 +21,8 @@
 NX, NH, NZ = 4, 2, 8
 NB = 4
 NEW = 4
-AT_ONCE = 4
+CUTS = 2
+AT_ONCE = 8
 
 
 def adam_update(weight_master, gradient, first_moment, second_moment):
@@ -35,7 +36,7 @@
     lengths, frequency, narrow, tokens, gain, bias, keys_in, values_in, context,
     W, A, N, ssq, psend, precv, J, cosine, sine, keys, values, mine, theirs,
     z_send, z_recv, x_send, x_recv, q_send, q_recv,
-    t_send, t_recv, s_send, s_recv, p_send, p_recv, e_send, e_recv, c_sem,
+    t1_send, t1_recv, t_send, t_recv, l_sem, s_send, s_recv, p_send, p_recv, e_send, e_recv, c_sem,
 ):
     heads, _, depth, lanes = W.shape
     rows = depth // NZ
@@ -73,11 +74,7 @@
 
     count, width = tokens.shape
     own_rows = count // NEW
-    to_row = lax.broadcasted_iota(jnp.int32, (count, count), 0)
-    to_col = lax.broadcasted_iota(jnp.int32, (count, count), 1)
-    order = (to_col == to_row % NEW * own_rows + to_row // NEW).astype(jnp.bfloat16)
-    back = (to_row == to_col % NEW * own_rows + to_col // NEW).astype(jnp.bfloat16)
-    flat = jnp.dot(order, tokens[...], preferred_element_type=jnp.float32)
+    flat = tokens[...].astype(jnp.float32)
     square = flat * flat
     part = square[:, :lanes]
     for k in range(1, square.shape[1] // lanes):
@@ -141,61 +138,88 @@
             arrive(w_group(j, (x + 2) % NX, g), x_send.at[j, 4 + g], x_recv.at[j, 4 + g],
                    x_up if g == 0 else x_down)
 
-    def a_at(b_, h_, s_):
-        return A.at[b_, 2 * h_ + s_]
+    cut_rows = count // CUTS
+
+    def a_at(b_, h_, s_, g=None):
+        rows_ = pl.ds(0, count) if g is None else pl.ds(g * cut_rows, cut_rows)
+        return A.at[2 * h_ + s_, rows_, pl.ds(pl.multiple_of(b_ * depth, 128), depth)]
+
+    def n_at(h_, s_, g):
+        return N.at[h_, s_, pl.ds(g * cut_rows, cut_rows)]
 
     local = []
     b_lo = (1 - lo) * 2 + c
 
-    def to_sibling(ref, kind, i):
-        send(ref, ref, s_send.at[kind, i], s_recv.at[kind, i], sibling)
-
-    def tokens_out(i, s_):
-        send(N.at[1 - h, s_], a_at(b, h, s_), t_send.at[0, i], t_recv.at[0, i], h_near)
-        send(N.at[h, s_], a_at(b, h, s_), t_send.at[1, i], t_recv.at[1, i], lo_pair)
-        own = pltpu.make_async_copy(N.at[h, s_], a_at(b, h, s_), t_recv.at[4, i])
+    def far_out(i, s_):
+        for g in range(CUTS):
+            send(n_at(1 - h, s_, g), a_at(b, h, s_, g), t_send.at[0, i, g], t_recv.at[0, i, g], h_near)
+
+    def near_out(i, s_, g):
+        send(n_at(h, s_, g), a_at(b, h, s_, g), t_send.at[1, i, g], t_recv.at[1, i, g], lo_pair)
+
+    def own_out(i, s_):
+        own = pltpu.make_async_copy(N.at[h, s_], a_at(b, h, s_), l_sem.at[i])
         own.start()
         local.append(own)
-        send(N.at[h, s_], a_at(b, h, s_), s_send.at[0, i], s_recv.at[0, i], sibling)
-
-    def tokens_on(i, s_):
-        piece = a_at(b_lo, 1 - h, s_)
-        arrive(piece, t_send.at[0, i], t_recv.at[0, i], h_near)
-        send(piece, piece, t_send.at[2, i], t_recv.at[2, i], lo_pair)
-        to_sibling(piece, 1, i)
-        piece = a_at(b_lo, h, s_)
-        arrive(piece, t_send.at[1, i], t_recv.at[1, i], lo_pair)
-        to_sibling(piece, 2, i)
-
-    def tokens_last(i, s_):
-        piece = a_at(b, 1 - h, s_)
-        arrive(piece, t_send.at[2, i], t_recv.at[2, i], lo_pair)
-        to_sibling(piece, 3, i)
+        send(N.at[h, s_], a_at(b, h, s_), s_send.at[0, i, 0], s_recv.at[0, i, 0], sibling)
+
+    def to_sibling(ref, kind, i, g):
+        send(ref, ref, s_send.at[kind, i, g], s_recv.at[kind, i, g], sibling)
+
+    def far_on(i, s_):
+        for g in range(CUTS):
+            piece = a_at(b_lo, 1 - h, s_, g)
+            arrive(piece, t_send.at[0, i, g], t_recv.at[0, i, g], h_near)
+            send(piece, piece, t_send.at[2, i, g], t_recv.at[2, i, g], lo_pair)
+            to_sibling(piece, 1, i, g)
+
+    def last_on(i, s_):
+        for kind, b_, h_ in ((1, b_lo, h), (2, b, 1 - h)):
+            for g in range(CUTS):
+                piece = a_at(b_, h_, s_, g)
+                arrive(piece, t_send.at[kind, i, g], t_recv.at[kind, i, g], lo_pair)
+                to_sibling(piece, kind + 1, i, g)
 
     def tokens_end():
         sib = lo * 2 + 1 - c
         sib_lo = (1 - lo) * 2 + 1 - c
         for i, s_ in ((0, s), (1, 1 - s)):
             local[i].wait()
-            for kind, b_, h_ in ((0, sib, h), (1, sib_lo, 1 - h), (2, sib_lo, h), (3, sib, 1 - h)):
-                arrive(a_at(b_, h_, s_), s_send.at[kind, i], s_recv.at[kind, i], sibling)
-
-    def project(j):
-        def block(m):
-            total = jnp.dot(A[0, m], W[j, 0], preferred_element_type=jnp.float32)
-            for b_ in range(1, NB):
-                total = total + jnp.dot(A[b_, m], W[j, b_], preferred_element_type=jnp.float32)
-            return total
-
-        @pl.loop(0, 2)
-        def _(s_):
-            psend[j, s_] = block(2 * (1 - h) + s_).astype(jnp.bfloat16)
-
-        send(psend.at[j], precv.at[j], p_send.at[j], p_recv.at[j], h_far)
-
-        @pl.loop(0, 2)
-        def _(s_):
-            J[j, s_] = block(2 * h + s_)
+            arrive(a_at(sib, h, s_), s_send.at[0, i, 0], s_recv.at[0, i, 0], sibling)
+            for kind, b_, h_ in ((1, sib_lo, 1 - h), (2, sib_lo, h), (3, sib, 1 - h)):
+                for g in range(CUTS):
+                    arrive(a_at(b_, h_, s_, g), s_send.at[kind, i, g], s_recv.at[kind, i, g], sibling)
+
+    full_depth = NB * depth
+
+    def project(group):
+        weights = [W[j].reshape(full_depth, lanes) for j in group]
+        weights = weights[0] if len(group) == 1 else jnp.concatenate(weights, axis=1)
+
+        def block(h_):
+            part = A[pl.ds(2 * h_, 2)].reshape(2 * count, full_depth)
+            return jnp.dot(part, weights, preferred_element_type=jnp.float32)
+
+        far = block(1 - h).astype(jnp.bfloat16)
+        for k, j in enumerate(group):
+            psend[j] = far[:, k * lanes : (k + 1) * lanes].reshape(2, count, lanes)
+            send(psend.at[j], precv.at[j], p_send.at[j], p_recv.at[j], h_far)
+        near = block(h)
+        for k, j in enumerate(group):
+            J[j] = near[:, k * lanes : (k + 1) * lanes].reshape(2, count, lanes)
+
+    queries = heads - 2
+    offsets = bias[...].astype(jnp.float32).reshape(1, 2 * heads * lanes)
+    offsets = jnp.where(s == 0, offsets[:, : heads * lanes], offsets[:, heads * lanes :])
+
+    def finish(j):
+        arrive(precv.at[j], p_send.at[j], p_recv.at[j], h_far)
+        offset = offsets[:, j * lanes : (j + 1) * lanes]
+        for s_ in (0, 1):
+            full = J[j, s_] + precv[j, s_].astype(jnp.float32) + offset
+            if j <= queries:
+                full = full * cosine[s_] + pltpu.roll(full, lanes // 2, 1) * sine[s_]
+            J[j, s_] = full.astype(jnp.bfloat16).astype(jnp.float32)
 
     own_lens = f // 2 * (2 * own_rows)
     two_rows = 2 * NEW
@@ -216,65 +240,75 @@
     for to, k in peers:
         send(ssq.at[b], ssq.at[b], q_send.at[k], q_recv.at[k], to)
     z_out(0)
-    z_out(1)
+    to_row = lax.broadcasted_iota(jnp.int32, (count, count), 0)
+    to_col = lax.broadcasted_iota(jnp.int32, (count, count), 1)
+    order = (to_col == to_row % NEW * own_rows + to_row // NEW).astype(jnp.bfloat16)
+    back = (to_row == to_col % NEW * own_rows + to_col // NEW).astype(jnp.bfloat16)
     for to, k in peers:
         arrive(ssq.at[(b // 2 * 2 + 1 - c) if k == 0 else (b_lo if k == 1 else (1 - lo) * 2 + 1 - c)],
                q_send.at[k], q_recv.at[k], to)
     total = ssq[0] + ssq[1] + ssq[2] + ssq[3]
     inverse = lax.rsqrt(jnp.sum(total, axis=1, keepdims=True) * (1.0 / (NB * width)) + NORM_EPS)
     gains = gain[...].astype(jnp.float32).reshape(1, width)
-    scaled = (flat * inverse * gains).astype(jnp.bfloat16)
+    scaled = (tokens[...].astype(jnp.float32) * inverse * gains).astype(jnp.bfloat16)
+    scaled = jnp.dot(order, scaled, preferred_element_type=jnp.float32).astype(jnp.bfloat16)
     N[0, s] = scaled[:, :depth]
     N[1, s] = scaled[:, depth:]
-    tokens_out(0, s)
-    send(N.at[1 - h, s], N.at[1 - h, s], t_send.at[3, 0], t_recv.at[3, 0], z_pair)
-    send(N.at[h, s], N.at[h, s], t_send.at[3, 1], t_recv.at[3, 1], z_pair)
+    send(N.at[1 - h, s], N.at[1 - h, s], t1_send.at[0], t1_recv.at[0], z_pair)
+    far_out(0, s)
+    send(N.at[h, s], N.at[h, s], t1_send.at[1], t1_recv.at[1], z_pair)
+    near_out(0, s, 0)
+    z_out(1)
+    own_out(0, s)
     x_out(0)
+    far_on(0, s)
+    near_out(0, s, 1)
     z_out(2)
     x_out(1)
     x_on(0)
+    arrive(N.at[1 - h, 1 - s], t1_send.at[0], t1_recv.at[0], z_pair)
+    far_out(1, 1 - s)
+    arrive(N.at[h, 1 - s], t1_send.at[1], t1_recv.at[1], z_pair)
+    near_out(1, 1 - s, 0)
+    own_out(1, 1 - s)
     z_out(3)
-    tokens_on(0, s)
-    for k, h_ in ((0, 1 - h), (1, h)):
-        arrive(N.at[h_, 1 - s], t_send.at[3, k], t_recv.at[3, k], z_pair)
-    tokens_out(1, 1 - s)
+    last_on(0, s)
     x_out(2)
-    tables(0)
     x_on(1)
     z_out(4)
-    tokens_last(0, s)
+    far_on(1, 1 - s)
+    near_out(1, 1 - s, 1)
+    tables(0)
     x_out(3)
-    tables(1)
     x_on(2)
     z_out(5)
-    tokens_on(1, 1 - s)
+    tables(1)
+    last_on(1, 1 - s)
     x_out(4)
     x_on(3)
     z_out(6)
     x_out(5)
     x_on(4)
-    tokens_last(1, 1 - s)
+    tokens_end()
+    x_end(0)
+    x_end(1)
+    project((0, 1))
     x_out(6)
-    tokens_end()
-    for j in range(heads):
-        if j == 3:
-            x_on(5)
-        if j == 5:
-            x_on(6)
-        x_end(j)
-        project(j)
+    x_on(5)
+    x_end(2)
+    x_end(3)
+    project((2, 3))
+    x_on(6)
+    x_end(4)
+    x_end(5)
+    project((4, 5))
+    for j in (0, 1, 2, 3):
+        finish(j)
+    x_end(6)
+    project((6,))
+    for j in (4, 5, 6):
+        finish(j)
     lens_at = f // 2 * (2 * own_rows)
-    queries = heads - 2
-    offsets = bias[...].astype(jnp.float32).reshape(1, 2 * heads * lanes)
-    offsets = jnp.where(s == 0, offsets[:, : heads * lanes], offsets[:, heads * lanes :])
-    for j in range(heads):
-        arrive(precv.at[j], p_send.at[j], p_recv.at[j], h_far)
-        offset = offsets[:, j * lanes : (j + 1) * lanes]
-        for s_ in (0, 1):
-            full = J[j, s_] + precv[j, s_].astype(jnp.float32) + offset
-            if j <= queries:
-                full = full * cosine[s_] + pltpu.roll(full, lanes // 2, 1) * sine[s_]
-            J[j, s_] = full.astype(jnp.bfloat16).astype(jnp.float32)
 
     for load in loads:
         load.wait()
@@ -368,7 +402,7 @@
         out_specs=vmem,
         scratch_shapes=[
             pltpu.VMEM((heads, NX, depth, lanes), jnp.bfloat16),
-            pltpu.VMEM((NB, 2 * NH, count, depth), jnp.bfloat16),
+            pltpu.VMEM((2 * NH, count, NB * depth), jnp.bfloat16),
             pltpu.VMEM((NH, 2, count, depth), jnp.bfloat16),
             pltpu.VMEM((NB, count, lanes), jnp.float32),
             pltpu.VMEM((heads, 2, count, lanes), jnp.bfloat16),
@@ -383,8 +417,10 @@
             dma((heads, NZ)), dma((heads, NZ)),
             dma((heads, 6)), dma((heads, 6)),
             dma((3,)), dma((3,)),
-            dma((5, 2)), dma((5, 2)),
-            dma((4, 2)), dma((4, 2)),
+            dma((2,)), dma((2,)),
+            dma((3, 2, CUTS)), dma((3, 2, CUTS)),
+            dma((2,)),
+            dma((4, 2, CUTS)), dma((4, 2, CUTS)),
             dma((heads,)), dma((heads,)),
             dma((2,)), dma((2,)), dma((2,)),
         ],

time: 96.3 us -> 103 us (1.070)
  Pallas kernels: 90.1 us -> 97.2 us
    pallas_call x1, Pallas kernels: 90.1 us -> 97.2 us  [project_tokens(): pl.pallas_call(layer_kernel, name='gather_project', out_shape=jax.ShapeDt...]
where the time goes in v3:
time: 103 us; the launch traced here: 102 us
  Pallas kernels  97.2 us (94%)
  other arithmetic  3.16 us (3%)
    pallas_call x1, Pallas kernels, project_tokens(): pl.pallas_call(layer_kernel, name='gather_project', out_shape=jax.ShapeDt...  97.2 us
    unnamed x1, other arithmetic  3.16 us

profile of v3, /device:TPU:32, one launch (start us, length us, event | category | flops | bytes accessed | tf_op | source)
XLA Modules:
  0.0 102.0 jit_solution(734462148447807877)
XLA Ops:
  0.6 0.0 copy-start.5
  0.6 0.0 copy-start
  0.7 0.0 copy-start.2
  0.7 0.0 copy-start.3
  0.7 0.0 copy-start.1
  0.7 0.0 copy-start.4
  0.7 3.2 %convert_bitcast_fusion = (bf16[10,14,8,128]{3,2,1,0:T(8,128)(2,1)S(1)}, f32[80,1792]{1,0:T(8,128)}, f32[80,1792]{1,0:T(8,128)}, f32[80,1792]{1,0:T(8,128)}) fusion(f32[80,1792]{1,0:T(8,128)} %param.11, f32[80,1792]{1,0:T(8,128)} %param.12, f32[80,1792]{1,0:T(8,128)} %param.13, f32[80,1792]{1,0:T(8,128)} %param.14), kind=kLoop, calls=%fused_computation.5 | loop fusion | flops 2007040 | bytes 4300800
  3.9 0.1 copy.18
  3.9 0.0 copy-done.5
  3.9 0.0 copy-done
  3.9 0.0 copy-done.2
  3.9 0.0 copy-done.3
  4.0 0.0 copy-done.1
  4.0 0.0 copy-done.4
  4.0 97.2 %gather_project.1 = bf16[192,1280]{1,0:T(8,128)(2,1)S(1)} custom-call(s32[3072]{0:T(1024)S(1)} %copy-done.2, f32[1,128]{1,0:T(1,128)S(1)} %copy-done.5, bf16[14,80,128]{2,1,0:T(8,128)(2,1)S(1)} %bitcast.13, bf16[192,1280]{1,0:T(8,128)(2,1)S(1)} %bitcast.15, bf16[1280]{0:T(1024)(128)(2,1)S(1)} %copy-done.3, bf16[1792]{0:T(1024)(128)(2,1)S(1)} %copy-done.4, ...), custom_call_target="tpu_custom_call" | custom-call | flops 3523215360 | bytes 12582912 | tf_op jit(solution)/shard_map/gather_project/pallas_call | solution.py:397
  101.2 0.8 copy.20
Async XLA Ops:
  0.6 3.3 %copy-start.5 = (f32[1,128]{1,0:T(1,128)S(1)}, f32[1,128]{1,0:T(1,128)}, u32[]{:S(2)}) copy-start(f32[1,128]{1,0:T(1,128)} %constant.20.clone.frequency) | copy-start | bytes 1540
  0.6 3.3 %copy-start = (bf16[1,1,96,160,128]{4,3,2,1,0:T(8,128)(2,1)S(1)}, bf16[1,1,96,160,128]{4,3,2,1,0:T(8,128)(2,1)}, u32[]{:S(2)}) copy-start(bf16[1,1,96,160,128]{4,3,2,1,0:T(8,128)(2,1)} %param.19) | copy-start | bytes 11796484
  0.7 3.3 %copy-start.2 = (s32[3072]{0:T(1024)S(1)}, s32[3072]{0:T(1024)}, u32[]{:S(2)}) copy-start(s32[3072]{0:T(1024)} %lengths.1) | copy-start | bytes 36868
  0.7 3.3 %copy-start.3 = (bf16[1280]{0:T(1024)(128)(2,1)S(1)}, bf16[1280]{0:T(1024)(128)(2,1)}, u32[]{:S(2)}) copy-start(bf16[1280]{0:T(1024)(128)(2,1)} %gain.1) | copy-start | bytes 7684
  0.7 3.3 %copy-start.1 = (bf16[4,48,1280]{2,1,0:T(8,128)(2,1)S(1)}, bf16[4,48,1280]{2,1,0:T(8,128)(2,1)}, u32[]{:S(2)}) copy-start(bf16[4,48,1280]{2,1,0:T(8,128)(2,1)} %param.16) | copy-start | bytes 1474564
  0.7 3.3 %copy-start.4 = (bf16[1792]{0:T(1024)(128)(2,1)S(1)}, bf16[1792]{0:T(1024)(128)(2,1)}, u32[]{:S(2)}) copy-start(bf16[1792]{0:T(1024)(128)(2,1)} %bias.1) | copy-start | bytes 10756

commit v4 on v3

--- a/solution.py
+++ b/solution.py
@@ -34,7 +34,7 @@
 
 def layer_kernel(
     lengths, frequency, narrow, tokens, gain, bias, keys_in, values_in, context,
-    W, A, N, ssq, psend, precv, J, cosine, sine, keys, values, mine, theirs,
+    W, A, N, R, ssq, tot, psend, precv, J, cosine, sine, keys, values, mine, theirs,
     z_send, z_recv, x_send, x_recv, q_send, q_recv,
     t1_send, t1_recv, t_send, t_recv, l_sem, s_send, s_recv, p_send, p_recv, e_send, e_recv, c_sem,
 ):
@@ -79,7 +79,9 @@
     part = square[:, :lanes]
     for k in range(1, square.shape[1] // lanes):
         part = part + square[:, k * lanes : (k + 1) * lanes]
-    ssq[b] = part
+    padded = ssq.shape[2]
+    part = jnp.concatenate([part, jnp.zeros((padded - count, lanes), jnp.float32)], axis=0)
+    ssq[b] = jnp.broadcast_to(jnp.sum(part.T, axis=0, keepdims=True), (8, padded))
     pl.semaphore_wait(barrier, len(everyone))
 
     sent = []
@@ -240,6 +242,9 @@
     for to, k in peers:
         send(ssq.at[b], ssq.at[b], q_send.at[k], q_recv.at[k], to)
     z_out(0)
+    for k, h_ in ((0, 1 - h), (1, h)):
+        raw = tokens.at[:, pl.ds(pl.multiple_of(h_ * depth, 128), depth)]
+        send(raw, R.at[h_], t1_send.at[k], t1_recv.at[k], z_pair)
     to_row = lax.broadcasted_iota(jnp.int32, (count, count), 0)
     to_col = lax.broadcasted_iota(jnp.int32, (count, count), 1)
     order = (to_col == to_row % NEW * own_rows + to_row // NEW).astype(jnp.bfloat16)
@@ -247,28 +252,41 @@
     for to, k in peers:
         arrive(ssq.at[(b // 2 * 2 + 1 - c) if k == 0 else (b_lo if k == 1 else (1 - lo) * 2 + 1 - c)],
                q_send.at[k], q_recv.at[k], to)
-    total = ssq[0] + ssq[1] + ssq[2] + ssq[3]
-    inverse = lax.rsqrt(jnp.sum(total, axis=1, keepdims=True) * (1.0 / (NB * width)) + NORM_EPS)
+    tot[0] = ssq[0] + ssq[1] + ssq[2] + ssq[3]
+    send(tot.at[0], tot.at[1], t1_send.at[2], t1_recv.at[2], z_pair)
+
+    def inverse_of(total):
+        inverse = lax.rsqrt(total * (1.0 / (NB * width)) + NORM_EPS)
+        return inverse.T[:count, :1]
+
     gains = gain[...].astype(jnp.float32).reshape(1, width)
-    scaled = (tokens[...].astype(jnp.float32) * inverse * gains).astype(jnp.bfloat16)
-    scaled = jnp.dot(order, scaled, preferred_element_type=jnp.float32).astype(jnp.bfloat16)
-    N[0, s] = scaled[:, :depth]
-    N[1, s] = scaled[:, depth:]
-    send(N.at[1 - h, s], N.at[1 - h, s], t1_send.at[0], t1_recv.at[0], z_pair)
+
+    def normalise(raw, inverse, gains_here):
+        scaled = (raw.astype(jnp.float32) * inverse * gains_here).astype(jnp.bfloat16)
+        return jnp.dot(order, scaled, preferred_element_type=jnp.float32).astype(jnp.bfloat16)
+
+    inverse = inverse_of(tot[0])
+    N[0, s] = normalise(tokens[:, :depth], inverse, gains[:, :depth])
+    N[1, s] = normalise(tokens[:, depth:], inverse, gains[:, depth:])
     far_out(0, s)
-    send(N.at[h, s], N.at[h, s], t1_send.at[1], t1_recv.at[1], z_pair)
     near_out(0, s, 0)
-    z_out(1)
     own_out(0, s)
     x_out(0)
+    z_out(1)
     far_on(0, s)
     near_out(0, s, 1)
-    z_out(2)
+    arrive(tot.at[1], t1_send.at[2], t1_recv.at[2], z_pair)
+    inverse = inverse_of(tot[1])
+    gains_near = jnp.where(h == 0, gains[:, :depth], gains[:, depth:])
+    gains_far = jnp.where(h == 0, gains[:, depth:], gains[:, :depth])
+    arrive(R.at[1 - h], t1_send.at[0], t1_recv.at[0], z_pair)
+    N[1 - h, 1 - s] = normalise(R[1 - h], inverse, gains_far)
+    far_out(1, 1 - s)
     x_out(1)
     x_on(0)
-    arrive(N.at[1 - h, 1 - s], t1_send.at[0], t1_recv.at[0], z_pair)
-    far_out(1, 1 - s)
-    arrive(N.at[h, 1 - s], t1_send.at[1], t1_recv.at[1], z_pair)
+    z_out(2)
+    arrive(R.at[h], t1_send.at[1], t1_recv.at[1], z_pair)
+    N[h, 1 - s] = normalise(R[h], inverse, gains_near)
     near_out(1, 1 - s, 0)
     own_out(1, 1 - s)
     z_out(3)
@@ -290,10 +308,10 @@
     x_out(5)
     x_on(4)
     tokens_end()
+    x_out(6)
     x_end(0)
     x_end(1)
     project((0, 1))
-    x_out(6)
     x_on(5)
     x_end(2)
     x_end(3)
@@ -389,6 +407,7 @@
     assert depth == NZ * rows
     piece = (heads - 2) * lanes
     half_lanes = lanes // 2
+    padded = -(-count // 128) * 128
     frequency = ROPE_BASE ** (-(np.arange(lanes) % half_lanes) / half_lanes)
     frequency = jnp.asarray(frequency.reshape(1, lanes), jnp.float32)
     dma = pltpu.SemaphoreType.DMA
@@ -404,7 +423,9 @@
             pltpu.VMEM((heads, NX, depth, lanes), jnp.bfloat16),
             pltpu.VMEM((2 * NH, count, NB * depth), jnp.bfloat16),
             pltpu.VMEM((NH, 2, count, depth), jnp.bfloat16),
-            pltpu.VMEM((NB, count, lanes), jnp.float32),
+            pltpu.VMEM((NH, count, depth), jnp.bfloat16),
+            pltpu.VMEM((NB, 8, padded), jnp.float32),
+            pltpu.VMEM((2, 8, padded), jnp.float32),
             pltpu.VMEM((heads, 2, count, lanes), jnp.bfloat16),
             pltpu.VMEM((heads, 2, count, lanes), jnp.bfloat16),
             pltpu.VMEM((heads, 2, count, lanes), jnp.float32),
@@ -417,7 +438,7 @@
             dma((heads, NZ)), dma((heads, NZ)),
             dma((heads, 6)), dma((heads, 6)),
             dma((3,)), dma((3,)),
-            dma((2,)), dma((2,)),
+            dma((3,)), dma((3,)),
             dma((3, 2, CUTS)), dma((3, 2, CUTS)),
             dma((2,)),
             dma((4, 2, CUTS)), dma((4, 2, CUTS)),

time: 103 us -> 98.2 us (0.953)
  Pallas kernels: 97.2 us -> 92.8 us
    pallas_call x1, Pallas kernels: 97.2 us -> 92.8 us  [project_tokens(): pl.pallas_call(layer_kernel, name='gather_project', out_shape=jax.ShapeDt...]
where the time goes in v4:
time: 98.2 us; the launch traced here: 97.5 us
  Pallas kernels  92.8 us (95%)
  other arithmetic  3.16 us (3%)
    pallas_call x1, Pallas kernels, project_tokens(): pl.pallas_call(layer_kernel, name='gather_project', out_shape=jax.ShapeDt...  92.8 us
    unnamed x1, other arithmetic  3.16 us

profile of v4, /device:TPU:32, one launch (start us, length us, event | category | flops | bytes accessed | tf_op | source)
XLA Modules:
  0.0 97.5 jit_solution(18254561913052193932)
XLA Ops:
  0.6 0.0 copy-start.5
  0.6 0.0 copy-start
  0.7 0.0 copy-start.2
  0.7 0.0 copy-start.3
  0.7 0.0 copy-start.1
  0.7 0.0 copy-start.4
  0.7 3.2 %convert_bitcast_fusion = (bf16[10,14,8,128]{3,2,1,0:T(8,128)(2,1)S(1)}, f32[80,1792]{1,0:T(8,128)}, f32[80,1792]{1,0:T(8,128)}, f32[80,1792]{1,0:T(8,128)}) fusion(f32[80,1792]{1,0:T(8,128)} %param.11, f32[80,1792]{1,0:T(8,128)} %param.12, f32[80,1792]{1,0:T(8,128)} %param.13, f32[80,1792]{1,0:T(8,128)} %param.14), kind=kLoop, calls=%fused_computation.5 | loop fusion | flops 2007040 | bytes 4300800
  3.9 0.1 copy.18
  3.9 0.0 copy-done.5
  3.9 0.0 copy-done
  3.9 0.0 copy-done.2
  3.9 0.0 copy-done.3
  4.0 0.0 copy-done.1
  4.0 0.0 copy-done.4
  4.0 92.8 %gather_project.1 = bf16[192,1280]{1,0:T(8,128)(2,1)S(1)} custom-call(s32[3072]{0:T(1024)S(1)} %copy-done.2, f32[1,128]{1,0:T(1,128)S(1)} %copy-done.5, bf16[14,80,128]{2,1,0:T(8,128)(2,1)S(1)} %bitcast.13, bf16[192,1280]{1,0:T(8,128)(2,1)S(1)} %bitcast.15, bf16[1280]{0:T(1024)(128)(2,1)S(1)} %copy-done.3, bf16[1792]{0:T(1024)(128)(2,1)S(1)} %copy-done.4, ...), custom_call_target="tpu_custom_call" | custom-call | flops 3523215360 | bytes 12582912 | tf_op jit(solution)/shard_map/gather_project/pallas_call | solution.py:416
  96.7 0.8 copy.20
Async XLA Ops:
  0.6 3.3 %copy-start.5 = (f32[1,128]{1,0:T(1,128)S(1)}, f32[1,128]{1,0:T(1,128)}, u32[]{:S(2)}) copy-start(f32[1,128]{1,0:T(1,128)} %constant.20.clone.frequency) | copy-start | bytes 1540
  0.6 3.3 %copy-start = (bf16[1,1,96,160,128]{4,3,2,1,0:T(8,128)(2,1)S(1)}, bf16[1,1,96,160,128]{4,3,2,1,0:T(8,128)(2,1)}, u32[]{:S(2)}) copy-start(bf16[1,1,96,160,128]{4,3,2,1,0:T(8,128)(2,1)} %param.19) | copy-start | bytes 11796484
  0.7 3.3 %copy-start.2 = (s32[3072]{0:T(1024)S(1)}, s32[3072]{0:T(1024)}, u32[]{:S(2)}) copy-start(s32[3072]{0:T(1024)} %lengths.1) | copy-start | bytes 36868
  0.7 3.3 %copy-start.3 = (bf16[1280]{0:T(1024)(128)(2,1)S(1)}, bf16[1280]{0:T(1024)(128)(2,1)}, u32[]{:S(2)}) copy-start(bf16[1280]{0:T(1024)(128)(2,1)} %gain.1) | copy-start | bytes 7684
  0.7 3.3 %copy-start.1 = (bf16[4,48,1280]{2,1,0:T(8,128)(2,1)S(1)}, bf16[4,48,1280]{2,1,0:T(8,128)(2,1)}, u32[]{:S(2)}) copy-start(bf16[4,48,1280]{2,1,0:T(8,128)(2,1)} %param.16) | copy-start | bytes 1474564
  0.7 3.3 %copy-start.4 = (bf16[1792]{0:T(1024)(128)(2,1)S(1)}, bf16[1792]{0:T(1024)(128)(2,1)}, u32[]{:S(2)}) copy-start(bf16[1792]{0:T(1024)(128)(2,1)} %bias.1) | copy-start | bytes 10756

commit v5 on v4

--- a/solution.py
+++ b/solution.py
@@ -144,7 +144,7 @@
 
     def a_at(b_, h_, s_, g=None):
         rows_ = pl.ds(0, count) if g is None else pl.ds(g * cut_rows, cut_rows)
-        return A.at[2 * h_ + s_, rows_, pl.ds(pl.multiple_of(b_ * depth, 128), depth)]
+        return A.at[b_, 2 * h_ + s_, rows_]
 
     def n_at(h_, s_, g):
         return N.at[h_, s_, pl.ds(g * cut_rows, cut_rows)]
@@ -192,15 +192,17 @@
                 for g in range(CUTS):
                     arrive(a_at(b_, h_, s_, g), s_send.at[kind, i, g], s_recv.at[kind, i, g], sibling)
 
-    full_depth = NB * depth
-
     def project(group):
-        weights = [W[j].reshape(full_depth, lanes) for j in group]
+        weights = [W[j].reshape(NB * depth, lanes) for j in group]
         weights = weights[0] if len(group) == 1 else jnp.concatenate(weights, axis=1)
 
         def block(h_):
-            part = A[pl.ds(2 * h_, 2)].reshape(2 * count, full_depth)
-            return jnp.dot(part, weights, preferred_element_type=jnp.float32)
+            total = None
+            for b_ in range(NB):
+                part = A[b_, pl.ds(2 * h_, 2)].reshape(2 * count, depth)
+                term = jnp.dot(part, weights[b_ * depth : (b_ + 1) * depth], preferred_element_type=jnp.float32)
+                total = term if total is None else total + term
+            return total
 
         far = block(1 - h).astype(jnp.bfloat16)
         for k, j in enumerate(group):
@@ -266,66 +268,73 @@
         return jnp.dot(order, scaled, preferred_element_type=jnp.float32).astype(jnp.bfloat16)
 
     inverse = inverse_of(tot[0])
-    N[0, s] = normalise(tokens[:, :depth], inverse, gains[:, :depth])
-    N[1, s] = normalise(tokens[:, depth:], inverse, gains[:, depth:])
+    gains_near = jnp.where(h == 0, gains[:, :depth], gains[:, depth:])
+    gains_far = jnp.where(h == 0, gains[:, depth:], gains[:, :depth])
+
+    def half_of(h_):
+        return tokens[:, pl.ds(pl.multiple_of(h_ * depth, 128), depth)]
+
+    N[1 - h, s] = normalise(half_of(1 - h), inverse, gains_far)
     far_out(0, s)
+    N[h, s] = normalise(half_of(h), inverse, gains_near)
     near_out(0, s, 0)
     own_out(0, s)
+    z_out(1)
     x_out(0)
-    z_out(1)
     far_on(0, s)
     near_out(0, s, 1)
+    z_out(2)
+    x_out(1)
     arrive(tot.at[1], t1_send.at[2], t1_recv.at[2], z_pair)
     inverse = inverse_of(tot[1])
-    gains_near = jnp.where(h == 0, gains[:, :depth], gains[:, depth:])
-    gains_far = jnp.where(h == 0, gains[:, depth:], gains[:, :depth])
     arrive(R.at[1 - h], t1_send.at[0], t1_recv.at[0], z_pair)
     N[1 - h, 1 - s] = normalise(R[1 - h], inverse, gains_far)
     far_out(1, 1 - s)
-    x_out(1)
-    x_on(0)
-    z_out(2)
+    z_out(3)
     arrive(R.at[h], t1_send.at[1], t1_recv.at[1], z_pair)
     N[h, 1 - s] = normalise(R[h], inverse, gains_near)
     near_out(1, 1 - s, 0)
     own_out(1, 1 - s)
-    z_out(3)
+    x_on(0)
+    x_out(2)
     last_on(0, s)
-    x_out(2)
-    x_on(1)
     z_out(4)
     far_on(1, 1 - s)
     near_out(1, 1 - s, 1)
+    x_on(1)
+    x_out(3)
+    z_out(5)
     tables(0)
-    x_out(3)
     x_on(2)
-    z_out(5)
+    x_out(4)
+    z_out(6)
+    last_on(1, 1 - s)
+    x_on(3)
+    x_out(5)
     tables(1)
-    last_on(1, 1 - s)
-    x_out(4)
-    x_on(3)
-    z_out(6)
-    x_out(5)
     x_on(4)
+    x_out(6)
     tokens_end()
-    x_out(6)
     x_end(0)
     x_end(1)
     project((0, 1))
-    x_on(5)
     x_end(2)
     x_end(3)
     project((2, 3))
+    x_on(5)
+    finish(0)
+    finish(1)
     x_on(6)
     x_end(4)
     x_end(5)
     project((4, 5))
-    for j in (0, 1, 2, 3):
-        finish(j)
+    finish(2)
+    finish(3)
     x_end(6)
     project((6,))
-    for j in (4, 5, 6):
-        finish(j)
+    finish(4)
+    finish(5)
+    finish(6)
     lens_at = f // 2 * (2 * own_rows)
 
     for load in loads:
@@ -421,7 +430,7 @@
         out_specs=vmem,
         scratch_shapes=[
             pltpu.VMEM((heads, NX, depth, lanes), jnp.bfloat16),
-            pltpu.VMEM((2 * NH, count, NB * depth), jnp.bfloat16),
+            pltpu.VMEM((NB, 2 * NH, count, depth), jnp.bfloat16),
             pltpu.VMEM((NH, 2, count, depth), jnp.bfloat16),
             pltpu.VMEM((NH, count, depth), jnp.bfloat16),
             pltpu.VMEM((NB, 8, padded), jnp.float32),

time: 98.2 us -> 98 us (level)
  no operation moved by 1% of the time
where the time goes in v5:
time: 98 us; the launch traced here: 97.9 us
  Pallas kernels  93.2 us (95%)
  other arithmetic  3.16 us (3%)
    pallas_call x1, Pallas kernels, project_tokens(): pl.pallas_call(layer_kernel, name='gather_project', out_shape=jax.ShapeDt...  93.2 us
    unnamed x1, other arithmetic  3.16 us

profile of v5, /device:TPU:32, one launch (start us, length us, event | category | flops | bytes accessed | tf_op | source)
XLA Modules:
  0.0 97.9 jit_solution(8743082554379993657)
XLA Ops:
  0.6 0.0 copy-start.5
  0.6 0.0 copy-start
  0.7 0.0 copy-start.2
  0.7 0.0 copy-start.3
  0.7 0.0 copy-start.1
  0.7 0.0 copy-start.4
  0.7 3.2 %convert_bitcast_fusion = (bf16[10,14,8,128]{3,2,1,0:T(8,128)(2,1)S(1)}, f32[80,1792]{1,0:T(8,128)}, f32[80,1792]{1,0:T(8,128)}, f32[80,1792]{1,0:T(8,128)}) fusion(f32[80,1792]{1,0:T(8,128)} %param.11, f32[80,1792]{1,0:T(8,128)} %param.12, f32[80,1792]{1,0:T(8,128)} %param.13, f32[80,1792]{1,0:T(8,128)} %param.14), kind=kLoop, calls=%fused_computation.5 | loop fusion | flops 2007040 | bytes 4300800
  3.9 0.1 copy.18
  3.9 0.0 copy-done.5
  3.9 0.0 copy-done
  3.9 0.0 copy-done.2
  3.9 0.0 copy-done.3
  4.0 0.0 copy-done.1
  4.0 0.0 copy-done.4
  4.0 93.2 %gather_project.1 = bf16[192,1280]{1,0:T(8,128)(2,1)S(1)} custom-call(s32[3072]{0:T(1024)S(1)} %copy-done.2, f32[1,128]{1,0:T(1,128)S(1)} %copy-done.5, bf16[14,80,128]{2,1,0:T(8,128)(2,1)S(1)} %bitcast.13, bf16[192,1280]{1,0:T(8,128)(2,1)S(1)} %bitcast.15, bf16[1280]{0:T(1024)(128)(2,1)S(1)} %copy-done.3, bf16[1792]{0:T(1024)(128)(2,1)S(1)} %copy-done.4, ...), custom_call_target="tpu_custom_call" | custom-call | flops 3523215360 | bytes 12582912 | tf_op jit(solution)/shard_map/gather_project/pallas_call | solution.py:425
  97.1 0.8 copy.20
Async XLA Ops:
  0.6 3.3 %copy-start.5 = (f32[1,128]{1,0:T(1,128)S(1)}, f32[1,128]{1,0:T(1,128)}, u32[]{:S(2)}) copy-start(f32[1,128]{1,0:T(1,128)} %constant.20.clone.frequency) | copy-start | bytes 1540
  0.6 3.3 %copy-start = (bf16[1,1,96,160,128]{4,3,2,1,0:T(8,128)(2,1)S(1)}, bf16[1,1,96,160,128]{4,3,2,1,0:T(8,128)(2,1)}, u32[]{:S(2)}) copy-start(bf16[1,1,96,160,128]{4,3,2,1,0:T(8,128)(2,1)} %param.19) | copy-start | bytes 11796484
  0.7 3.3 %copy-start.2 = (s32[3072]{0:T(1024)S(1)}, s32[3072]{0:T(1024)}, u32[]{:S(2)}) copy-start(s32[3072]{0:T(1024)} %lengths.1) | copy-start | bytes 36868
  0.7 3.3 %copy-start.3 = (bf16[1280]{0:T(1024)(128)(2,1)S(1)}, bf16[1280]{0:T(1024)(128)(2,1)}, u32[]{:S(2)}) copy-start(bf16[1280]{0:T(1024)(128)(2,1)} %gain.1) | copy-start | bytes 7684
  0.7 3.3 %copy-start.1 = (bf16[4,48,1280]{2,1,0:T(8,128)(2,1)S(1)}, bf16[4,48,1280]{2,1,0:T(8,128)(2,1)}, u32[]{:S(2)}) copy-start(bf16[4,48,1280]{2,1,0:T(8,128)(2,1)} %param.16) | copy-start | bytes 1474564
  0.7 3.3 %copy-start.4 = (bf16[1792]{0:T(1024)(128)(2,1)S(1)}, bf16[1792]{0:T(1024)(128)(2,1)}, u32[]{:S(2)}) copy-start(bf16[1792]{0:T(1024)(128)(2,1)} %bias.1) | copy-start | bytes 10756

commit v6 on v2

--- a/solution.py
+++ b/solution.py
@@ -21,7 +21,7 @@
 NX, NH, NZ = 4, 2, 8
 NB = 4
 NEW = 4
-AT_ONCE = 4
+AT_ONCE = 8
 
 
 def adam_update(weight_master, gradient, first_moment, second_moment):
@@ -73,16 +73,14 @@
 
     count, width = tokens.shape
     own_rows = count // NEW
-    to_row = lax.broadcasted_iota(jnp.int32, (count, count), 0)
-    to_col = lax.broadcasted_iota(jnp.int32, (count, count), 1)
-    order = (to_col == to_row % NEW * own_rows + to_row // NEW).astype(jnp.bfloat16)
-    back = (to_row == to_col % NEW * own_rows + to_col // NEW).astype(jnp.bfloat16)
-    flat = jnp.dot(order, tokens[...], preferred_element_type=jnp.float32)
+    flat = tokens[...].astype(jnp.float32)
     square = flat * flat
     part = square[:, :lanes]
     for k in range(1, square.shape[1] // lanes):
         part = part + square[:, k * lanes : (k + 1) * lanes]
-    ssq[b] = part
+    padded = ssq.shape[2]
+    part = jnp.concatenate([part, jnp.zeros((padded - count, lanes), jnp.float32)], axis=0)
+    ssq[b] = jnp.broadcast_to(jnp.sum(part.T, axis=0, keepdims=True), (8, padded))
     pl.semaphore_wait(barrier, len(everyone))
 
     sent = []
@@ -180,22 +178,38 @@
             for kind, b_, h_ in ((0, sib, h), (1, sib_lo, 1 - h), (2, sib_lo, h), (3, sib, 1 - h)):
                 arrive(a_at(b_, h_, s_), s_send.at[kind, i], s_recv.at[kind, i], sibling)
 
-    def project(j):
-        def block(m):
-            total = jnp.dot(A[0, m], W[j, 0], preferred_element_type=jnp.float32)
-            for b_ in range(1, NB):
-                total = total + jnp.dot(A[b_, m], W[j, b_], preferred_element_type=jnp.float32)
+    def project(group):
+        weights = [W[j].reshape(NB * depth, lanes) for j in group]
+        weights = weights[0] if len(group) == 1 else jnp.concatenate(weights, axis=1)
+
+        def block(h_):
+            total = None
+            for b_ in range(NB):
+                part = A[b_, pl.ds(2 * h_, 2)].reshape(2 * count, depth)
+                term = jnp.dot(part, weights[b_ * depth : (b_ + 1) * depth], preferred_element_type=jnp.float32)
+                total = term if total is None else total + term
             return total
 
-        @pl.loop(0, 2)
-        def _(s_):
-            psend[j, s_] = block(2 * (1 - h) + s_).astype(jnp.bfloat16)
-
-        send(psend.at[j], precv.at[j], p_send.at[j], p_recv.at[j], h_far)
-
-        @pl.loop(0, 2)
-        def _(s_):
-            J[j, s_] = block(2 * h + s_)
+        far = block(1 - h).astype(jnp.bfloat16)
+        for k, j in enumerate(group):
+            psend[j] = far[:, k * lanes : (k + 1) * lanes].reshape(2, count, lanes)
+            send(psend.at[j], precv.at[j], p_send.at[j], p_recv.at[j], h_far)
+        near = block(h)
+        for k, j in enumerate(group):
+            J[j] = near[:, k * lanes : (k + 1) * lanes].reshape(2, count, lanes)
+
+    queries = heads - 2
+    offsets = bias[...].astype(jnp.float32).reshape(1, 2 * heads * lanes)
+    offsets = jnp.where(s == 0, offsets[:, : heads * lanes], offsets[:, heads * lanes :])
+
+    def finish(j):
+        arrive(precv.at[j], p_send.at[j], p_recv.at[j], h_far)
+        offset = offsets[:, j * lanes : (j + 1) * lanes]
+        for s_ in (0, 1):
+            full = J[j, s_] + precv[j, s_].astype(jnp.float32) + offset
+            if j <= queries:
+                full = full * cosine[s_] + pltpu.roll(full, lanes // 2, 1) * sine[s_]
+            J[j, s_] = full.astype(jnp.bfloat16).astype(jnp.float32)
 
     own_lens = f // 2 * (2 * own_rows)
     two_rows = 2 * NEW
@@ -217,13 +231,18 @@
         send(ssq.at[b], ssq.at[b], q_send.at[k], q_recv.at[k], to)
     z_out(0)
     z_out(1)
+    to_row = lax.broadcasted_iota(jnp.int32, (count, count), 0)
+    to_col = lax.broadcasted_iota(jnp.int32, (count, count), 1)
+    order = (to_col == to_row % NEW * own_rows + to_row // NEW).astype(jnp.bfloat16)
+    back = (to_row == to_col % NEW * own_rows + to_col // NEW).astype(jnp.bfloat16)
     for to, k in peers:
         arrive(ssq.at[(b // 2 * 2 + 1 - c) if k == 0 else (b_lo if k == 1 else (1 - lo) * 2 + 1 - c)],
                q_send.at[k], q_recv.at[k], to)
     total = ssq[0] + ssq[1] + ssq[2] + ssq[3]
-    inverse = lax.rsqrt(jnp.sum(total, axis=1, keepdims=True) * (1.0 / (NB * width)) + NORM_EPS)
+    inverse = lax.rsqrt(total * (1.0 / (NB * width)) + NORM_EPS).T[:count, :1]
     gains = gain[...].astype(jnp.float32).reshape(1, width)
-    scaled = (flat * inverse * gains).astype(jnp.bfloat16)
+    scaled = (tokens[...].astype(jnp.float32) * inverse * gains).astype(jnp.bfloat16)
+    scaled = jnp.dot(order, scaled, preferred_element_type=jnp.float32).astype(jnp.bfloat16)
     N[0, s] = scaled[:, :depth]
     N[1, s] = scaled[:, depth:]
     tokens_out(0, s)
@@ -256,25 +275,27 @@
     tokens_last(1, 1 - s)
     x_out(6)
     tokens_end()
-    for j in range(heads):
-        if j == 3:
-            x_on(5)
-        if j == 5:
-            x_on(6)
-        x_end(j)
-        project(j)
+    x_end(0)
+    x_end(1)
+    project((0, 1))
+    x_on(5)
+    x_end(2)
+    x_end(3)
+    project((2, 3))
+    finish(0)
+    finish(1)
+    x_on(6)
+    x_end(4)
+    x_end(5)
+    project((4, 5))
+    finish(2)
+    finish(3)
+    x_end(6)
+    project((6,))
+    finish(4)
+    finish(5)
+    finish(6)
     lens_at = f // 2 * (2 * own_rows)
-    queries = heads - 2
-    offsets = bias[...].astype(jnp.float32).reshape(1, 2 * heads * lanes)
-    offsets = jnp.where(s == 0, offsets[:, : heads * lanes], offsets[:, heads * lanes :])
-    for j in range(heads):
-        arrive(precv.at[j], p_send.at[j], p_recv.at[j], h_far)
-        offset = offsets[:, j * lanes : (j + 1) * lanes]
-        for s_ in (0, 1):
-            full = J[j, s_] + precv[j, s_].astype(jnp.float32) + offset
-            if j <= queries:
-                full = full * cosine[s_] + pltpu.roll(full, lanes // 2, 1) * sine[s_]
-            J[j, s_] = full.astype(jnp.bfloat16).astype(jnp.float32)
 
     for load in loads:
         load.wait()
@@ -355,6 +376,7 @@
     assert depth == NZ * rows
     piece = (heads - 2) * lanes
     half_lanes = lanes // 2
+    padded = -(-count // 128) * 128
     frequency = ROPE_BASE ** (-(np.arange(lanes) % half_lanes) / half_lanes)
     frequency = jnp.asarray(frequency.reshape(1, lanes), jnp.float32)
     dma = pltpu.SemaphoreType.DMA
@@ -370,7 +392,7 @@
             pltpu.VMEM((heads, NX, depth, lanes), jnp.bfloat16),
             pltpu.VMEM((NB, 2 * NH, count, depth), jnp.bfloat16),
             pltpu.VMEM((NH, 2, count, depth), jnp.bfloat16),
-            pltpu.VMEM((NB, count, lanes), jnp.float32),
+            pltpu.VMEM((NB, 8, padded), jnp.float32),
             pltpu.VMEM((heads, 2, count, lanes), jnp.bfloat16),
             pltpu.VMEM((heads, 2, count, lanes), jnp.bfloat16),
             pltpu.VMEM((heads, 2, count, lanes), jnp.float32),

time: 96.3 us -> 95.7 us (level); the launches traced: 94.9 us -> 95.5 us
  no operation moved by 1% of the time
where the time goes in v6:
time: 95.7 us; the launch traced here: 95.5 us
  Pallas kernels  90.8 us (95%)
  other arithmetic  3.16 us (3%)
    pallas_call x1, Pallas kernels, project_tokens(): pl.pallas_call(layer_kernel, name='gather_project', out_shape=jax.ShapeDt...  90.8 us
    unnamed x1, other arithmetic  3.16 us

profile of v6, /device:TPU:32, one launch (start us, length us, event | category | flops | bytes accessed | tf_op | source)
XLA Modules:
  0.0 95.5 jit_solution(9137257605352256801)
XLA Ops:
  0.6 0.0 copy-start.5
  0.6 0.0 copy-start
  0.7 0.0 copy-start.2
  0.7 0.0 copy-start.3
  0.7 0.0 copy-start.1
  0.7 0.0 copy-start.4
  0.7 3.2 %convert_bitcast_fusion = (bf16[10,14,8,128]{3,2,1,0:T(8,128)(2,1)S(1)}, f32[80,1792]{1,0:T(8,128)}, f32[80,1792]{1,0:T(8,128)}, f32[80,1792]{1,0:T(8,128)}) fusion(f32[80,1792]{1,0:T(8,128)} %param.11, f32[80,1792]{1,0:T(8,128)} %param.12, f32[80,1792]{1,0:T(8,128)} %param.13, f32[80,1792]{1,0:T(8,128)} %param.14), kind=kLoop, calls=%fused_computation.5 | loop fusion | flops 2007040 | bytes 4300800
  3.9 0.1 copy.18
  3.9 0.0 copy-done.5
  3.9 0.0 copy-done
  3.9 0.0 copy-done.2
  3.9 0.0 copy-done.3
  4.0 0.0 copy-done.1
  4.0 0.0 copy-done.4
  4.0 90.8 %gather_project.1 = bf16[192,1280]{1,0:T(8,128)(2,1)S(1)} custom-call(s32[3072]{0:T(1024)S(1)} %copy-done.2, f32[1,128]{1,0:T(1,128)S(1)} %copy-done.5, bf16[14,80,128]{2,1,0:T(8,128)(2,1)S(1)} %bitcast.13, bf16[192,1280]{1,0:T(8,128)(2,1)S(1)} %bitcast.15, bf16[1280]{0:T(1024)(128)(2,1)S(1)} %copy-done.3, bf16[1792]{0:T(1024)(128)(2,1)S(1)} %copy-done.4, ...), custom_call_target="tpu_custom_call" | custom-call | flops 3523215360 | bytes 12582912 | tf_op jit(solution)/shard_map/gather_project/pallas_call | solution.py:385
  94.7 0.8 copy.20
Async XLA Ops:
  0.6 3.3 %copy-start.5 = (f32[1,128]{1,0:T(1,128)S(1)}, f32[1,128]{1,0:T(1,128)}, u32[]{:S(2)}) copy-start(f32[1,128]{1,0:T(1,128)} %constant.20.clone.frequency) | copy-start | bytes 1540
  0.6 3.3 %copy-start = (bf16[1,1,96,160,128]{4,3,2,1,0:T(8,128)(2,1)S(1)}, bf16[1,1,96,160,128]{4,3,2,1,0:T(8,128)(2,1)}, u32[]{:S(2)}) copy-start(bf16[1,1,96,160,128]{4,3,2,1,0:T(8,128)(2,1)} %param.19) | copy-start | bytes 11796484
  0.7 3.3 %copy-start.2 = (s32[3072]{0:T(1024)S(1)}, s32[3072]{0:T(1024)}, u32[]{:S(2)}) copy-start(s32[3072]{0:T(1024)} %lengths.1) | copy-start | bytes 36868
  0.7 3.3 %copy-start.3 = (bf16[1280]{0:T(1024)(128)(2,1)S(1)}, bf16[1280]{0:T(1024)(128)(2,1)}, u32[]{:S(2)}) copy-start(bf16[1280]{0:T(1024)(128)(2,1)} %gain.1) | copy-start | bytes 7684
  0.7 3.3 %copy-start.1 = (bf16[4,48,1280]{2,1,0:T(8,128)(2,1)S(1)}, bf16[4,48,1280]{2,1,0:T(8,128)(2,1)}, u32[]{:S(2)}) copy-start(bf16[4,48,1280]{2,1,0:T(8,128)(2,1)} %param.16) | copy-start | bytes 1474564
  0.7 3.3 %copy-start.4 = (bf16[1792]{0:T(1024)(128)(2,1)S(1)}, bf16[1792]{0:T(1024)(128)(2,1)}, u32[]{:S(2)}) copy-start(bf16[1792]{0:T(1024)(128)(2,1)} %bias.1) | copy-start | bytes 10756

commit v7 on v6

--- a/solution.py
+++ b/solution.py
@@ -111,14 +111,20 @@
         own = pltpu.make_async_copy(narrow.at[s * heads + j], w_rows(j, x, z), z_recv.at[j, 0])
         own.start()
         own_copies[j] = own
-        for d in (4, 3, 5, 2, 6, 1, 7):
+        for d in (1, 7, 2, 6):
             parity = (s + d) % 2
             send(narrow.at[parity * heads + j], w_rows(j, x, z), z_send.at[j, d],
                  z_recv.at[j, d], z_to[d])
 
+    def z_on(j):
+        for d, onward, to in ((1, 3, 2), (7, 5, 6), (2, 4, 2) if j % 2 == 0 else (6, 4, 6)):
+            block = w_rows(j, x, (z + NZ - d) % NZ)
+            arrive(block, z_send.at[j, d], z_recv.at[j, d], z_to[d])
+            send(block, block, z_send.at[j, onward], z_recv.at[j, onward], z_to[to])
+
     def x_out(j):
         own_copies[j].wait()
-        for d in range(1, NZ):
+        for d in (3, 4, 5, 6 if j % 2 == 0 else 2):
             arrive(w_rows(j, x, (z + NZ - d) % NZ), z_send.at[j, d], z_recv.at[j, d], z_to[d])
         for g in (0, 1):
             for k, to in ((0, x_up), (1, x_down)):
@@ -238,6 +244,7 @@
     for to, k in peers:
         arrive(ssq.at[(b // 2 * 2 + 1 - c) if k == 0 else (b_lo if k == 1 else (1 - lo) * 2 + 1 - c)],
                q_send.at[k], q_recv.at[k], to)
+    z_on(0)
     total = ssq[0] + ssq[1] + ssq[2] + ssq[3]
     inverse = lax.rsqrt(total * (1.0 / (NB * width)) + NORM_EPS).T[:count, :1]
     gains = gain[...].astype(jnp.float32).reshape(1, width)
@@ -249,28 +256,34 @@
     send(N.at[1 - h, s], N.at[1 - h, s], t_send.at[3, 0], t_recv.at[3, 0], z_pair)
     send(N.at[h, s], N.at[h, s], t_send.at[3, 1], t_recv.at[3, 1], z_pair)
     x_out(0)
+    z_on(1)
     z_out(2)
     x_out(1)
     x_on(0)
+    z_on(2)
     z_out(3)
     tokens_on(0, s)
     for k, h_ in ((0, 1 - h), (1, h)):
         arrive(N.at[h_, 1 - s], t_send.at[3, k], t_recv.at[3, k], z_pair)
     tokens_out(1, 1 - s)
     x_out(2)
+    z_on(3)
+    z_out(4)
     tables(0)
     x_on(1)
-    z_out(4)
     tokens_last(0, s)
     x_out(3)
+    z_on(4)
+    z_out(5)
     tables(1)
     x_on(2)
-    z_out(5)
     tokens_on(1, 1 - s)
     x_out(4)
+    z_on(5)
+    z_out(6)
     x_on(3)
-    z_out(6)
     x_out(5)
+    z_on(6)
     x_on(4)
     tokens_last(1, 1 - s)
     x_out(6)

time: 95.7 us -> 95.8 us (level)
  no operation moved by 1% of the time
where the time goes in v7:
time: 95.8 us; the launch traced here: 95.7 us
  Pallas kernels  91 us (95%)
  other arithmetic  3.16 us (3%)
    pallas_call x1, Pallas kernels, project_tokens(): pl.pallas_call(layer_kernel, name='gather_project', out_shape=jax.ShapeDt...  91 us
    unnamed x1, other arithmetic  3.16 us

profile of v7, /device:TPU:32, one launch (start us, length us, event | category | flops | bytes accessed | tf_op | source)
XLA Modules:
  0.0 95.7 jit_solution(13670936469041530826)
XLA Ops:
  0.6 0.0 copy-start.5
  0.6 0.0 copy-start
  0.7 0.0 copy-start.2
  0.7 0.0 copy-start.3
  0.7 0.0 copy-start.1
  0.7 0.0 copy-start.4
  0.7 3.2 %convert_bitcast_fusion = (bf16[10,14,8,128]{3,2,1,0:T(8,128)(2,1)S(1)}, f32[80,1792]{1,0:T(8,128)}, f32[80,1792]{1,0:T(8,128)}, f32[80,1792]{1,0:T(8,128)}) fusion(f32[80,1792]{1,0:T(8,128)} %param.11, f32[80,1792]{1,0:T(8,128)} %param.12, f32[80,1792]{1,0:T(8,128)} %param.13, f32[80,1792]{1,0:T(8,128)} %param.14), kind=kLoop, calls=%fused_computation.5 | loop fusion | flops 2007040 | bytes 4300800
  3.9 0.1 copy.18
  3.9 0.0 copy-done.5
  3.9 0.0 copy-done
  3.9 0.0 copy-done.2
  3.9 0.0 copy-done.3
  4.0 0.0 copy-done.1
  4.0 0.0 copy-done.4
  4.0 91.0 %gather_project.1 = bf16[192,1280]{1,0:T(8,128)(2,1)S(1)} custom-call(s32[3072]{0:T(1024)S(1)} %copy-done.2, f32[1,128]{1,0:T(1,128)S(1)} %copy-done.5, bf16[14,80,128]{2,1,0:T(8,128)(2,1)S(1)} %bitcast.13, bf16[192,1280]{1,0:T(8,128)(2,1)S(1)} %bitcast.15, bf16[1280]{0:T(1024)(128)(2,1)S(1)} %copy-done.3, bf16[1792]{0:T(1024)(128)(2,1)S(1)} %copy-done.4, ...), custom_call_target="tpu_custom_call" | custom-call | flops 3523215360 | bytes 12582912 | tf_op jit(solution)/shard_map/gather_project/pallas_call | solution.py:398
  95.0 0.8 copy.20
Async XLA Ops:
  0.6 3.3 %copy-start.5 = (f32[1,128]{1,0:T(1,128)S(1)}, f32[1,128]{1,0:T(1,128)}, u32[]{:S(2)}) copy-start(f32[1,128]{1,0:T(1,128)} %constant.20.clone.frequency) | copy-start | bytes 1540
  0.6 3.3 %copy-start = (bf16[1,1,96,160,128]{4,3,2,1,0:T(8,128)(2,1)S(1)}, bf16[1,1,96,160,128]{4,3,2,1,0:T(8,128)(2,1)}, u32[]{:S(2)}) copy-start(bf16[1,1,96,160,128]{4,3,2,1,0:T(8,128)(2,1)} %param.19) | copy-start | bytes 11796484
  0.7 3.3 %copy-start.2 = (s32[3072]{0:T(1024)S(1)}, s32[3072]{0:T(1024)}, u32[]{:S(2)}) copy-start(s32[3072]{0:T(1024)} %lengths.1) | copy-start | bytes 36868
  0.7 3.3 %copy-start.3 = (bf16[1280]{0:T(1024)(128)(2,1)S(1)}, bf16[1280]{0:T(1024)(128)(2,1)}, u32[]{:S(2)}) copy-start(bf16[1280]{0:T(1024)(128)(2,1)} %gain.1) | copy-start | bytes 7684
  0.7 3.3 %copy-start.1 = (bf16[4,48,1280]{2,1,0:T(8,128)(2,1)S(1)}, bf16[4,48,1280]{2,1,0:T(8,128)(2,1)}, u32[]{:S(2)}) copy-start(bf16[4,48,1280]{2,1,0:T(8,128)(2,1)} %param.16) | copy-start | bytes 1474564
  0.7 3.3 %copy-start.4 = (bf16[1792]{0:T(1024)(128)(2,1)S(1)}, bf16[1792]{0:T(1024)(128)(2,1)}, u32[]{:S(2)}) copy-start(bf16[1792]{0:T(1024)(128)(2,1)} %bias.1) | copy-start | bytes 10756

commit v8 on v5

--- a/solution.py
+++ b/solution.py
@@ -112,14 +112,20 @@
         own = pltpu.make_async_copy(narrow.at[s * heads + j], w_rows(j, x, z), z_recv.at[j, 0])
         own.start()
         own_copies[j] = own
-        for d in (4, 3, 5, 2, 6, 1, 7):
+        for d in (1, 7, 2, 6):
             parity = (s + d) % 2
             send(narrow.at[parity * heads + j], w_rows(j, x, z), z_send.at[j, d],
                  z_recv.at[j, d], z_to[d])
 
+    def z_on(j):
+        for d, onward, to in ((1, 3, 2), (7, 5, 6), (2, 4, 2) if j % 2 == 0 else (6, 4, 6)):
+            block = w_rows(j, x, (z + NZ - d) % NZ)
+            arrive(block, z_send.at[j, d], z_recv.at[j, d], z_to[d])
+            send(block, block, z_send.at[j, onward], z_recv.at[j, onward], z_to[to])
+
     def x_out(j):
         own_copies[j].wait()
-        for d in range(1, NZ):
+        for d in (3, 4, 5, 6 if j % 2 == 0 else 2):
             arrive(w_rows(j, x, (z + NZ - d) % NZ), z_send.at[j, d], z_recv.at[j, d], z_to[d])
         for g in (0, 1):
             for k, to in ((0, x_up), (1, x_down)):
@@ -267,6 +273,7 @@
         scaled = (raw.astype(jnp.float32) * inverse * gains_here).astype(jnp.bfloat16)
         return jnp.dot(order, scaled, preferred_element_type=jnp.float32).astype(jnp.bfloat16)
 
+    z_on(0)
     inverse = inverse_of(tot[0])
     gains_near = jnp.where(h == 0, gains[:, :depth], gains[:, depth:])
     gains_far = jnp.where(h == 0, gains[:, depth:], gains[:, :depth])
@@ -276,41 +283,47 @@
 
     N[1 - h, s] = normalise(half_of(1 - h), inverse, gains_far)
     far_out(0, s)
+    z_out(1)
     N[h, s] = normalise(half_of(h), inverse, gains_near)
     near_out(0, s, 0)
     own_out(0, s)
-    z_out(1)
     x_out(0)
+    z_on(1)
+    z_out(2)
     far_on(0, s)
     near_out(0, s, 1)
-    z_out(2)
     x_out(1)
+    z_on(2)
+    z_out(3)
     arrive(tot.at[1], t1_send.at[2], t1_recv.at[2], z_pair)
     inverse = inverse_of(tot[1])
     arrive(R.at[1 - h], t1_send.at[0], t1_recv.at[0], z_pair)
     N[1 - h, 1 - s] = normalise(R[1 - h], inverse, gains_far)
     far_out(1, 1 - s)
-    z_out(3)
     arrive(R.at[h], t1_send.at[1], t1_recv.at[1], z_pair)
     N[h, 1 - s] = normalise(R[h], inverse, gains_near)
     near_out(1, 1 - s, 0)
     own_out(1, 1 - s)
     x_on(0)
     x_out(2)
+    z_on(3)
+    z_out(4)
     last_on(0, s)
-    z_out(4)
     far_on(1, 1 - s)
     near_out(1, 1 - s, 1)
     x_on(1)
     x_out(3)
+    z_on(4)
     z_out(5)
     tables(0)
     x_on(2)
     x_out(4)
+    z_on(5)
     z_out(6)
     last_on(1, 1 - s)
     x_on(3)
     x_out(5)
+    z_on(6)
     tables(1)
     x_on(4)
     x_out(6)

time: 98 us -> 96.4 us (0.984)
  Pallas kernels: 93.2 us -> 91 us
    pallas_call x1, Pallas kernels: 93.2 us -> 91 us  [project_tokens(): pl.pallas_call(layer_kernel, name='gather_project', out_shape=jax.ShapeDt...]
where the time goes in v8:
time: 96.4 us; the launch traced here: 95.8 us
  Pallas kernels  91 us (94%)
  other arithmetic  3.16 us (3%)
    pallas_call x1, Pallas kernels, project_tokens(): pl.pallas_call(layer_kernel, name='gather_project', out_shape=jax.ShapeDt...  91 us
    unnamed x1, other arithmetic  3.16 us

profile of v8, /device:TPU:32, one launch (start us, length us, event | category | flops | bytes accessed | tf_op | source)
XLA Modules:
  0.0 95.8 jit_solution(11940255396392687445)
XLA Ops:
  0.6 0.0 copy-start.5
  0.6 0.0 copy-start
  0.7 0.0 copy-start.2
  0.7 0.0 copy-start.3
  0.7 0.0 copy-start.1
  0.7 0.0 copy-start.4
  0.7 3.2 %convert_bitcast_fusion = (bf16[10,14,8,128]{3,2,1,0:T(8,128)(2,1)S(1)}, f32[80,1792]{1,0:T(8,128)}, f32[80,1792]{1,0:T(8,128)}, f32[80,1792]{1,0:T(8,128)}) fusion(f32[80,1792]{1,0:T(8,128)} %param.11, f32[80,1792]{1,0:T(8,128)} %param.12, f32[80,1792]{1,0:T(8,128)} %param.13, f32[80,1792]{1,0:T(8,128)} %param.14), kind=kLoop, calls=%fused_computation.5 | loop fusion | flops 2007040 | bytes 4300800
  3.9 0.1 copy.18
  3.9 0.0 copy-done.5
  3.9 0.0 copy-done
  3.9 0.0 copy-done.2
  3.9 0.0 copy-done.3
  4.0 0.0 copy-done.1
  4.0 0.0 copy-done.4
  4.0 91.0 %gather_project.1 = bf16[192,1280]{1,0:T(8,128)(2,1)S(1)} custom-call(s32[3072]{0:T(1024)S(1)} %copy-done.2, f32[1,128]{1,0:T(1,128)S(1)} %copy-done.5, bf16[14,80,128]{2,1,0:T(8,128)(2,1)S(1)} %bitcast.13, bf16[192,1280]{1,0:T(8,128)(2,1)S(1)} %bitcast.15, bf16[1280]{0:T(1024)(128)(2,1)S(1)} %copy-done.3, bf16[1792]{0:T(1024)(128)(2,1)S(1)} %copy-done.4, ...), custom_call_target="tpu_custom_call" | custom-call | flops 3523215360 | bytes 12582912 | tf_op jit(solution)/shard_map/gather_project/pallas_call | solution.py:438
  95.0 0.8 copy.20
Async XLA Ops:
  0.6 3.3 %copy-start.5 = (f32[1,128]{1,0:T(1,128)S(1)}, f32[1,128]{1,0:T(1,128)}, u32[]{:S(2)}) copy-start(f32[1,128]{1,0:T(1,128)} %constant.20.clone.frequency) | copy-start | bytes 1540
  0.6 3.3 %copy-start = (bf16[1,1,96,160,128]{4,3,2,1,0:T(8,128)(2,1)S(1)}, bf16[1,1,96,160,128]{4,3,2,1,0:T(8,128)(2,1)}, u32[]{:S(2)}) copy-start(bf16[1,1,96,160,128]{4,3,2,1,0:T(8,128)(2,1)} %param.19) | copy-start | bytes 11796484
  0.7 3.3 %copy-start.2 = (s32[3072]{0:T(1024)S(1)}, s32[3072]{0:T(1024)}, u32[]{:S(2)}) copy-start(s32[3072]{0:T(1024)} %lengths.1) | copy-start | bytes 36868
  0.7 3.3 %copy-start.3 = (bf16[1280]{0:T(1024)(128)(2,1)S(1)}, bf16[1280]{0:T(1024)(128)(2,1)}, u32[]{:S(2)}) copy-start(bf16[1280]{0:T(1024)(128)(2,1)} %gain.1) | copy-start | bytes 7684
  0.7 3.3 %copy-start.1 = (bf16[4,48,1280]{2,1,0:T(8,128)(2,1)S(1)}, bf16[4,48,1280]{2,1,0:T(8,128)(2,1)}, u32[]{:S(2)}) copy-start(bf16[4,48,1280]{2,1,0:T(8,128)(2,1)} %param.16) | copy-start | bytes 1474564
  0.7 3.3 %copy-start.4 = (bf16[1792]{0:T(1024)(128)(2,1)S(1)}, bf16[1792]{0:T(1024)(128)(2,1)}, u32[]{:S(2)}) copy-start(bf16[1792]{0:T(1024)(128)(2,1)} %bias.1) | copy-start | bytes 10756

commit v9 on v7

--- a/solution.py
+++ b/solution.py
@@ -252,10 +252,10 @@
     scaled = jnp.dot(order, scaled, preferred_element_type=jnp.float32).astype(jnp.bfloat16)
     N[0, s] = scaled[:, :depth]
     N[1, s] = scaled[:, depth:]
+    x_out(0)
     tokens_out(0, s)
     send(N.at[1 - h, s], N.at[1 - h, s], t_send.at[3, 0], t_recv.at[3, 0], z_pair)
     send(N.at[h, s], N.at[h, s], t_send.at[3, 1], t_recv.at[3, 1], z_pair)
-    x_out(0)
     z_on(1)
     z_out(2)
     x_out(1)
@@ -285,8 +285,8 @@
     x_out(5)
     z_on(6)
     x_on(4)
+    x_out(6)
     tokens_last(1, 1 - s)
-    x_out(6)
     tokens_end()
     x_end(0)
     x_end(1)

time: 95.8 us -> 99.2 us (1.035)
  Pallas kernels: 91 us -> 93.4 us
    pallas_call x1, Pallas kernels: 91 us -> 93.4 us  [project_tokens(): pl.pallas_call(layer_kernel, name='gather_project', out_shape=jax.ShapeDt...]
where the time goes in v9:
time: 99.2 us; the launch traced here: 98.2 us
  Pallas kernels  93.4 us (94%)
  other arithmetic  3.16 us (3%)
    pallas_call x1, Pallas kernels, project_tokens(): pl.pallas_call(layer_kernel, name='gather_project', out_shape=jax.ShapeDt...  93.4 us
    unnamed x1, other arithmetic  3.16 us

profile of v9, /device:TPU:32, one launch (start us, length us, event | category | flops | bytes accessed | tf_op | source)
XLA Modules:
  0.0 98.2 jit_solution(10323907255124103961)
XLA Ops:
  0.6 0.0 copy-start.5
  0.6 0.0 copy-start
  0.7 0.0 copy-start.2
  0.7 0.0 copy-start.3
  0.7 0.0 copy-start.1
  0.7 0.0 copy-start.4
  0.7 3.2 %convert_bitcast_fusion = (bf16[10,14,8,128]{3,2,1,0:T(8,128)(2,1)S(1)}, f32[80,1792]{1,0:T(8,128)}, f32[80,1792]{1,0:T(8,128)}, f32[80,1792]{1,0:T(8,128)}) fusion(f32[80,1792]{1,0:T(8,128)} %param.11, f32[80,1792]{1,0:T(8,128)} %param.12, f32[80,1792]{1,0:T(8,128)} %param.13, f32[80,1792]{1,0:T(8,128)} %param.14), kind=kLoop, calls=%fused_computation.5 | loop fusion | flops 2007040 | bytes 4300800
  3.9 0.1 copy.18
  3.9 0.0 copy-done.5
  3.9 0.0 copy-done
  3.9 0.0 copy-done.2
  3.9 0.0 copy-done.3
  4.0 0.0 copy-done.1
  4.0 0.0 copy-done.4
  4.0 93.4 %gather_project.1 = bf16[192,1280]{1,0:T(8,128)(2,1)S(1)} custom-call(s32[3072]{0:T(1024)S(1)} %copy-done.2, f32[1,128]{1,0:T(1,128)S(1)} %copy-done.5, bf16[14,80,128]{2,1,0:T(8,128)(2,1)S(1)} %bitcast.13, bf16[192,1280]{1,0:T(8,128)(2,1)S(1)} %bitcast.15, bf16[1280]{0:T(1024)(128)(2,1)S(1)} %copy-done.3, bf16[1792]{0:T(1024)(128)(2,1)S(1)} %copy-done.4, ...), custom_call_target="tpu_custom_call" | custom-call | flops 3523215360 | bytes 12582912 | tf_op jit(solution)/shard_map/gather_project/pallas_call | solution.py:398
  97.4 0.8 copy.20
Async XLA Ops:
  0.6 3.3 %copy-start.5 = (f32[1,128]{1,0:T(1,128)S(1)}, f32[1,128]{1,0:T(1,128)}, u32[]{:S(2)}) copy-start(f32[1,128]{1,0:T(1,128)} %constant.20.clone.frequency) | copy-start | bytes 1540
  0.6 3.3 %copy-start = (bf16[1,1,96,160,128]{4,3,2,1,0:T(8,128)(2,1)S(1)}, bf16[1,1,96,160,128]{4,3,2,1,0:T(8,128)(2,1)}, u32[]{:S(2)}) copy-start(bf16[1,1,96,160,128]{4,3,2,1,0:T(8,128)(2,1)} %param.19) | copy-start | bytes 11796484
  0.7 3.3 %copy-start.2 = (s32[3072]{0:T(1024)S(1)}, s32[3072]{0:T(1024)}, u32[]{:S(2)}) copy-start(s32[3072]{0:T(1024)} %lengths.1) | copy-start | bytes 36868
  0.7 3.3 %copy-start.3 = (bf16[1280]{0:T(1024)(128)(2,1)S(1)}, bf16[1280]{0:T(1024)(128)(2,1)}, u32[]{:S(2)}) copy-start(bf16[1280]{0:T(1024)(128)(2,1)} %gain.1) | copy-start | bytes 7684
  0.7 3.3 %copy-start.1 = (bf16[4,48,1280]{2,1,0:T(8,128)(2,1)S(1)}, bf16[4,48,1280]{2,1,0:T(8,128)(2,1)}, u32[]{:S(2)}) copy-start(bf16[4,48,1280]{2,1,0:T(8,128)(2,1)} %param.16) | copy-start | bytes 1474564
  0.7 3.3 %copy-start.4 = (bf16[1792]{0:T(1024)(128)(2,1)S(1)}, bf16[1792]{0:T(1024)(128)(2,1)}, u32[]{:S(2)}) copy-start(bf16[1792]{0:T(1024)(128)(2,1)} %bias.1) | copy-start | bytes 10756
